TPU v7x, 32 devices: a whole 2x2x4 slice. The times are simulated.
32 devices in a mesh: dp: 16 (over z, y, core), mp: 2 (over x).
Axes of the slice: x: 2, y: 2, z: 4, core: 2. Of those that a mesh axis runs over, the one named last changes fastest.
Arguments:
- tokens: bfloat16 [35840, 1024], P(('dp', 'mp')), may hold values from -6 to 6
- cond_flags: int32 [32, 3], P('dp'), may hold values 0 or 1
- seg_lengths: int32 [32, 3], P('dp'), may hold values from 1 to 560, 1120 in all within a row
- norm_gains: float32 [4, 1024], replicated, may hold values from 0.5 to 1.5
- norm_biases: float32 [4, 1024], replicated, may hold values from -3 to 3
- w_qkv: bfloat16 [3, 1024, 1024], P(None, None, 'mp'), may hold values from -0.25 to 0.25
- qv_bias: float32 [2, 1024], P(None, 'mp'), may hold values from -3 to 3
- w_out: bfloat16 [1024, 1024], P('mp'), may hold values from -0.1875 to 0.1875
- out_biases: float32 [2, 1024], replicated, may hold values from -3 to 3
- w_up: bfloat16 [1024, 4096], P(None, 'mp'), may hold values from -0.1875 to 0.1875
- up_bias: float32 [4096], P('mp'), may hold values from -3 to 3
- w_down: bfloat16 [4096, 1024], P('mp'), may hold values from -0.09375 to 0.09375
- cotangent: bfloat16 [35840, 1024], P(('dp', 'mp')), may hold values from -6 to 6
Outputs:
- output: bfloat16 [35840, 1024], P(('dp', 'mp'))
- grad_input: float32 [35840, 1024], P(('dp', 'mp'))
- grad_norm_gains: float32 [4, 1024], replicated
- grad_norm_biases: float32 [4, 1024], replicated
- grad_w_qkv: float32 [3, 1024, 1024], P(None, None, 'mp')
- grad_qv_bias: float32 [2, 1024], P(None, 'mp')
- grad_w_out: float32 [1024, 1024], P('mp')
- grad_out_biases: float32 [2, 1024], replicated
- grad_w_up: float32 [1024, 4096], P(None, 'mp')
- grad_up_bias: float32 [4096], P('mp')
- grad_w_down: float32 [4096, 1024], P('mp')
Inputs may be any that keep to these rules, and one draw needn't show every extreme that they name: `cond_flags`: 1 marks a segment whose tokens are conditioning. `seg_lengths`: a sequence's segment lengths in order (text, low-resolution codes, high-resolution patch codes); they sum to 1120, and the longest is exactly half of 1120.
All inputs are finite; a program needn't handle non-finite values. No bound on the sum of `cond_flags` on one device may be relied on, other than what follows from the above.
Results may differ from a plain program's by a relative error of at most 0.02.
Values may be sent and summed in bfloat16 or wider, within the bound.
A program may use at most 320 MiB of HBM per device.

v0:
```python
from functools import partial
import math

import jax
import jax.numpy as jnp
from jax import lax
from jax.sharding import PartitionSpec as P

HD = 64


epsilon = 1e-05
relax_factor = 32.0


def standardize(entries):
    average = jnp.mean(entries, axis=-1, keepdims=True)
    centred = entries - average
    spread = jnp.mean(centred * centred, axis=-1, keepdims=True)
    inv_std = lax.rsqrt(spread + epsilon)
    return (centred * inv_std, inv_std)


def norm_back(grad_in, normed, inv_std, gain_row):
    weighted = grad_in * gain_row
    return inv_std * (
        weighted
        - jnp.mean(weighted, axis=-1, keepdims=True)
        - normed * jnp.mean(weighted * normed, axis=-1, keepdims=True)
    )


def token_marks(seg_flags, lengths, length):
    position = jnp.arange(length, dtype=jnp.int32)
    segment = (position >= lengths[0]).astype(jnp.int32) + (
        position >= lengths[0] + lengths[1]
    ).astype(jnp.int32)
    segment_hits = (segment[:, None] == jnp.arange(3, dtype=jnp.int32)[None, :]).astype(jnp.int32)
    return jnp.sum(segment_hits * seg_flags[None, :], axis=1)


def block_mask(marks_seq, first_row, block_rows, length):
    query_places = first_row + jnp.arange(block_rows, dtype=jnp.int32)
    key_places = jnp.arange(length, dtype=jnp.int32)
    return (key_places[None, :] <= query_places[:, None]) | (marks_seq[None, :] == 1)


def shards(
    tokens,
    cond_flags,
    seg_lengths,
    norm_gains,
    norm_biases,
    w_qkv,
    qv_bias,
    w_out,
    out_biases,
    w_up,
    up_bias,
    w_down,
    cotangent,
):
    shard_rows = tokens.shape[0]
    group_rows = shard_rows * lax.axis_size("mp")
    seq_count = cond_flags.shape[0]
    length = group_rows // seq_count
    block_rows = length // 2
    head_count = w_qkv.shape[2] // HD
    local_width = head_count * HD
    query_scale = 1.0 / (relax_factor * math.sqrt(HD))
    all_marks = jax.vmap(lambda seg_flags, lengths: token_marks(seg_flags, lengths, length))(
        cond_flags, seg_lengths
    )
    numbers = jnp.arange(seq_count * 2, dtype=jnp.int32)
    source = tokens.astype(jnp.float32)
    normed_one, scale_one = standardize(source)
    first_in = (normed_one * norm_gains[0] + norm_biases[0]).astype(jnp.bfloat16)
    first_all = lax.all_gather(first_in, "mp", axis=0, tiled=True)
    bias_rows = jnp.stack([qv_bias[0], jnp.zeros_like(qv_bias[0]), qv_bias[1]])
    projected = (
        jnp.einsum("td,cde->cte", first_all, w_qkv, preferred_element_type=jnp.float32)
        + bias_rows[:, None, :]
    )
    queries = (
        (projected[0] * query_scale)
        .astype(jnp.bfloat16)
        .reshape(seq_count * 2, block_rows, head_count, HD)
    )
    key_all = projected[1].astype(jnp.bfloat16).reshape(seq_count, length, head_count, HD)
    value_all = projected[2].astype(jnp.bfloat16).reshape(seq_count, length, head_count, HD)

    def block_probs(query_block, number, row_top, row_total):
        sequence = number // 2
        first_row = number % 2 * block_rows
        key_seq = lax.dynamic_index_in_dim(key_all, sequence, 0, keepdims=False)
        allowed = block_mask(
            lax.dynamic_index_in_dim(all_marks, sequence, 0, keepdims=False),
            first_row,
            block_rows,
            length,
        )
        scores = jnp.einsum(
            "qhd,khd->hqk", query_block, key_seq, preferred_element_type=jnp.float32
        )
        if row_top is None:
            row_top = jnp.max(jnp.where(allowed[None], scores, -1e30), axis=-1, keepdims=True)
        weights = jnp.exp(jnp.where(allowed[None], (scores - row_top) * relax_factor, -30000.0))
        if row_total is None:
            row_total = jnp.sum(weights, axis=-1, keepdims=True)
        return (weights / row_total, row_top, row_total, key_seq)

    def forward_block(block_item):
        query_block, number = block_item
        probs, row_top, row_total, key_seq = block_probs(query_block, number, None, None)
        value_seq = lax.dynamic_index_in_dim(value_all, number // 2, 0, keepdims=False)
        mixed_block = jnp.einsum(
            "hqk,khd->qhd",
            probs.astype(jnp.bfloat16),
            value_seq,
            preferred_element_type=jnp.float32,
        )
        return (mixed_block.astype(jnp.bfloat16), row_top, row_total)

    mixed_heads, row_tops, row_totals = lax.map(forward_block, (queries, numbers))
    mixed_heads = mixed_heads.reshape(group_rows, local_width)
    attended = (
        lax.psum_scatter(
            jnp.dot(mixed_heads, w_out, preferred_element_type=jnp.float32),
            "mp",
            scatter_dimension=0,
            tiled=True,
        )
        + out_biases[0]
    )
    normed_two, scale_two = standardize(attended)
    residual = source + normed_two * norm_gains[1] + norm_biases[1]
    normed_three, scale_three = standardize(residual)
    third_in = (normed_three * norm_gains[2] + norm_biases[2]).astype(jnp.bfloat16)
    third_all = lax.all_gather(third_in, "mp", axis=0, tiled=True)
    up_value = jnp.dot(third_all, w_up, preferred_element_type=jnp.float32) + up_bias
    activated = jax.nn.gelu(up_value, approximate=True).astype(jnp.bfloat16)
    down = (
        lax.psum_scatter(
            jnp.dot(activated, w_down, preferred_element_type=jnp.float32),
            "mp",
            scatter_dimension=0,
            tiled=True,
        )
        + out_biases[1]
    )
    normed_four, scale_four = standardize(down)
    result = (residual + normed_four * norm_gains[3] + norm_biases[3]).astype(jnp.bfloat16)
    grad_out = cotangent.astype(jnp.float32)
    d_down = norm_back(grad_out, normed_four, scale_four, norm_gains[3])
    d_down_low = d_down.astype(jnp.bfloat16)
    d_down_all = lax.all_gather(d_down_low, "mp", axis=0, tiled=True)
    d_act = jnp.einsum("td,fd->tf", d_down_all, w_down, preferred_element_type=jnp.float32)
    grad_w_down = jnp.einsum("tf,td->fd", activated, d_down_all, preferred_element_type=jnp.float32)
    gelu_value, gelu_pull = jax.vjp(partial(jax.nn.gelu, approximate=True), up_value)
    d_up = gelu_pull(d_act)[0].astype(jnp.bfloat16)
    grad_w_up = jnp.einsum("td,tf->df", third_all, d_up, preferred_element_type=jnp.float32)
    grad_up_bias = jnp.sum(d_up, axis=0, dtype=jnp.float32)
    d_third = lax.psum_scatter(
        jnp.einsum("tf,df->td", d_up, w_up, preferred_element_type=jnp.float32),
        "mp",
        scatter_dimension=0,
        tiled=True,
    )
    d_residual = grad_out + norm_back(d_third, normed_three, scale_three, norm_gains[2])
    d_attended = norm_back(d_residual, normed_two, scale_two, norm_gains[1])
    d_att_low = d_attended.astype(jnp.bfloat16)
    d_att_all = lax.all_gather(d_att_low, "mp", axis=0, tiled=True)
    d_mixed = jnp.einsum("td,hd->th", d_att_all, w_out, preferred_element_type=jnp.float32).astype(
        jnp.bfloat16
    )
    grad_w_out = jnp.einsum("th,td->hd", mixed_heads, d_att_all, preferred_element_type=jnp.float32)
    d_mixed_blocks = d_mixed.reshape(seq_count * 2, block_rows, head_count, HD)

    def backward_block(block_item):
        query_block, d_block, row_top, row_total, number = block_item
        probs, kept_top, kept_total, key_seq = block_probs(query_block, number, row_top, row_total)
        value_seq = lax.dynamic_index_in_dim(value_all, number // 2, 0, keepdims=False)
        d_probs = jnp.einsum("qhd,khd->hqk", d_block, value_seq, preferred_element_type=jnp.float32)
        inner = jnp.sum(probs * d_probs, axis=-1, keepdims=True)
        d_scores = (relax_factor * probs * (d_probs - inner)).astype(jnp.bfloat16)
        d_query = (
            jnp.einsum("hqk,khd->qhd", d_scores, key_seq, preferred_element_type=jnp.float32)
            * query_scale
        )
        d_key = jnp.einsum(
            "hqk,qhd->khd", d_scores, query_block, preferred_element_type=jnp.float32
        )
        d_value = jnp.einsum(
            "hqk,qhd->khd", probs.astype(jnp.bfloat16), d_block, preferred_element_type=jnp.float32
        )
        return (d_query.astype(jnp.bfloat16), d_key, d_value)

    d_queries, d_keys, d_values = lax.map(
        backward_block, (queries, d_mixed_blocks, row_tops, row_totals, numbers)
    )
    d_keys = jnp.sum(d_keys.reshape(seq_count, 2, length, local_width), axis=1).reshape(
        group_rows, local_width
    )
    d_values = jnp.sum(d_values.reshape(seq_count, 2, length, local_width), axis=1).reshape(
        group_rows, local_width
    )
    d_qkv = jnp.stack(
        [
            d_queries.reshape(group_rows, local_width),
            d_keys.astype(jnp.bfloat16),
            d_values.astype(jnp.bfloat16),
        ]
    )
    grad_w_qkv = jnp.einsum("td,cte->cde", first_all, d_qkv, preferred_element_type=jnp.float32)
    grad_qv_bias = jnp.stack(
        [jnp.sum(d_qkv[0], axis=0, dtype=jnp.float32), jnp.sum(d_qkv[2], axis=0, dtype=jnp.float32)]
    )
    d_first = lax.psum_scatter(
        jnp.einsum("cte,cde->td", d_qkv, w_qkv, preferred_element_type=jnp.float32).astype(
            jnp.bfloat16
        ),
        "mp",
        scatter_dimension=0,
        tiled=True,
    ).astype(jnp.float32)
    grad_input = d_residual + norm_back(d_first, normed_one, scale_one, norm_gains[0])
    error_terms = (d_first, d_residual, d_third, grad_out)
    normed_terms = (normed_one, normed_two, normed_three, normed_four)
    gain_sums = jnp.stack(
        [
            jnp.sum(error_term * normed_term, axis=0)
            for error_term, normed_term in zip(error_terms, normed_terms)
        ]
    )
    bias_sums = jnp.stack([jnp.sum(error_term, axis=0) for error_term in error_terms])
    outer_sums = jnp.stack([jnp.sum(d_attended, axis=0), jnp.sum(d_down, axis=0)])
    gain_sums, bias_sums, outer_sums = lax.psum((gain_sums, bias_sums, outer_sums), ("dp", "mp"))
    grad_w_qkv, grad_qv_bias, grad_w_out, grad_w_up, grad_up_bias, grad_w_down = (
        lax.psum(grad_w_qkv.astype(jnp.bfloat16), "dp").astype(jnp.float32),
        lax.psum(grad_qv_bias.astype(jnp.bfloat16), "dp").astype(jnp.float32),
        lax.psum(grad_w_out.astype(jnp.bfloat16), "dp").astype(jnp.float32),
        lax.psum(grad_w_up.astype(jnp.bfloat16), "dp").astype(jnp.float32),
        lax.psum(grad_up_bias.astype(jnp.bfloat16), "dp").astype(jnp.float32),
        lax.psum(grad_w_down.astype(jnp.bfloat16), "dp").astype(jnp.float32),
    )
    return (
        result,
        grad_input,
        gain_sums,
        bias_sums,
        grad_w_qkv,
        grad_qv_bias,
        grad_w_out,
        outer_sums,
        grad_w_up,
        grad_up_bias,
        grad_w_down,
    )


def solution(mesh):
    in_specs = (
        P(("dp", "mp"), None),
        P("dp", None),
        P("dp", None),
        P(),
        P(),
        P(None, None, "mp"),
        P(None, "mp"),
        P("mp", None),
        P(),
        P(None, "mp"),
        P("mp"),
        P("mp", None),
        P(("dp", "mp"), None),
    )
    out_specs = (
        P(("dp", "mp"), None),
        P(("dp", "mp"), None),
        P(),
        P(),
        P(None, None, "mp"),
        P(None, "mp"),
        P("mp", None),
        P(),
        P(None, "mp"),
        P("mp"),
        P("mp", None),
    )
    return jax.shard_map(shards, mesh=mesh, in_specs=in_specs, out_specs=out_specs, check_vma=False)
```

profile of v0, /device:TPU:0, one launch (start us, length us, event | category | flops | bytes accessed | tf_op | source)
XLA Modules:
  0.0 1602.9 jit_solution(17422603232568903470)
XLA Ops:
  16.2 63.3 %all-gather.5.cloned.1.call-done = bf16[2240,1024]{1,0:T(8,128)(2,1)} async-done(((bf16[1120,1024]{1,0:T(8,128)(2,1)}), bf16[2240,1024]{1,0:T(8,128)(2,1)}) %all-gather.5.cloned.1.call-update) | async-done | bytes 4587536 | tf_op jit(solution)/shard_map/all_gather | solution.py:78
  79.6 12.1 fusion.100
  139.3 134.3 %while.32 = (s32[]{:T(128)}, bf16[4,560,8,64]{1,3,2,0:T(8,128)(2,1)}, f32[4,8,560,1]{2,1,3,0:T(8,128)}, f32[4,8,560,1]{2,1,3,0:T(8,128)}, s32[4]{0:T(128)S(1)}, ...) while((s32[]{:T(128)}, ...), condition=%wide.region_6.7_spmd, body=%wide.region_3.6_spmd.sunk | while | flops 1341233152 | bytes 147423104 | solution.py:124
  293.7 107.2 %reduce-scatter.5.cloned.1.call-done = f32[1120,1024]{1,0:T(8,128)} async-done(((f32[2240,1024]{1,0:T(8,128)}), f32[1120,1024]{1,0:T(8,128)}) %reduce-scatter.5.cloned.1.call-update) | async-done | bytes 4587536 | tf_op jit(solution)/shard_map/reduce_scatter | solution.py:127
  411.4 61.3 %all-gather.7.cloned.1.call-done = bf16[2240,1024]{1,0:T(8,128)(2,1)} async-done(((bf16[1120,1024]{1,0:T(8,128)(2,1)}), bf16[2240,1024]{1,0:T(8,128)(2,1)}) %all-gather.7.cloned.1.call-update) | async-done | bytes 4587536 | tf_op jit(solution)/shard_map/all_gather | solution.py:139
  472.7 20.1 %multiply_convert_fusion.1 = (bf16[2240,2048]{1,0:T(8,128)(2,1)S(1)}, f32[2240,2048]{1,0:T(8,128)}) fusion(f32[2048]{0:T(1024)S(1)} %copy-done.46, bf16[2240,1024]{1,0:T(8,128)(2,1)} %all-gather.7.cloned.1.call-done, bf16[1024,2048]{1,0:T(8,128)(2,1)} %param.26), kind=kOutput, calls=%fused_computation.73 | convolution fusion | flops 9441116160 | bytes 36315136 | tf_op jit(solution)/shard_map/dot_general | solution.py:140
  496.3 12.1 fusion.103
  508.8 107.4 %reduce-scatter.7.cloned.1.call-done = f32[1120,1024]{1,0:T(8,128)} async-done(((f32[2240,1024]{1,0:T(8,128)}), f32[1120,1024]{1,0:T(8,128)}) %reduce-scatter.7.cloned.1.call-update) | async-done | bytes 4587536 | tf_op jit(solution)/shard_map/reduce_scatter | solution.py:143
  627.9 61.3 %all-gather.9.cloned.1.call-done = bf16[2240,1024]{1,0:T(8,128)(2,1)} async-done(((bf16[1120,1024]{1,0:T(8,128)(2,1)}), bf16[2240,1024]{1,0:T(8,128)(2,1)}) %all-gather.9.cloned.1.call-update) | async-done | bytes 4587536 | tf_op jit(solution)/shard_map/all_gather | solution.py:156
  689.2 27.8 %fusion.101 = (bf16[2048]{0:T(1024)(128)(2,1)}, bf16[2240,2048]{1,0:T(8,128)(2,1)}) fusion(f32[2240,2048]{1,0:T(8,128)} %get-tuple-element.551, f32[2048]{0:T(1024)S(1)} %copy-done.46, bf16[2240,1024]{1,0:T(8,128)(2,1)} %all-gather.9.cloned.1.call-done, bf16[2048,1024]{1,0:T(8,128)(2,1)} %param.28), kind=kOutput, calls=%fused_computation.176 | convolution fusion | flops 9496164352 | bytes 36319232 | tf_op jit(solution)/shard_map/td,fd->tf/dot_general | solution.py:157
  717.0 14.5 fusion.104
  731.7 107.7 %reduce-scatter.9.cloned.1.call-done = f32[1120,1024]{1,0:T(8,128)} async-done(((f32[2240,1024]{1,0:T(8,128)}), f32[1120,1024]{1,0:T(8,128)}) %reduce-scatter.9.cloned.1.call-update) | async-done | bytes 4587536 | tf_op jit(solution)/shard_map/reduce_scatter | solution.py:163
  856.7 15.3 convolution_convert_fusion.1
  872.0 15.3 convolution_convert_fusion.2
  887.3 30.6 %all-gather.11.cloned.1.call-done = bf16[2240,1024]{1,0:T(8,128)(2,1)} async-done(((bf16[1120,1024]{1,0:T(8,128)(2,1)}), bf16[2240,1024]{1,0:T(8,128)(2,1)}) %all-gather.11.cloned.1.call-update) | async-done | bytes 4587536 | tf_op jit(solution)/shard_map/all_gather | solution.py:172
  939.4 258.6 %while.33 = (s32[]{:T(128)}, bf16[4,560,8,64]{1,3,2,0:T(8,128)(2,1)}, f32[4,1120,8,64]{1,3,2,0:T(8,128)}, f32[4,1120,8,64]{1,3,2,0:T(8,128)}, s32[4]{0:T(128)S(1...) while((s32[]{:T(128)}, ...), condition=%wide.region_24.25_spmd, body=%wide.region_22.24_spmd.sunk | while | flops 3268282624 | bytes 174082448 | solution.py:198
  944.3 11.3 fusion.156
  955.6 16.0 multiply_reduce_fusion.11
  971.6 13.6 multiply_convert_fusion.3
  1008.8 11.4 fusion.156
  1020.1 16.0 multiply_reduce_fusion.11
  1036.1 13.6 multiply_convert_fusion.3
  1073.3 11.4 fusion.156
  1084.7 16.0 multiply_reduce_fusion.11
  1100.7 13.6 multiply_convert_fusion.3
  1137.9 11.3 fusion.156
  1149.2 16.0 multiply_reduce_fusion.11
  1165.2 13.6 multiply_convert_fusion.3
  1265.3 36.1 %all-reduce.1 = (bf16[2,512]{1,0:T(2,128)(2,1)S(1)}, bf16[2048]{0:T(1024)(128)(2,1)S(1)}) all-reduce(bf16[2,512]{1,0:T(2,128)(2,1)S(1)} %pad_maximum_fusion.9, bf16[2048]{0:T(1024)(128)(2,1)S(1)} %copy-done.40), channel_id=1, replica_groups=mesh['dp'=16,'mp'=2] {'dp'}, use_global_device_ids=true, to_apply=%region_43.44 | all-reduce | flops 3072 | bytes 12288 | tf_op jit(solution)/shard_map/psum | solution.py:240
  1302.6 182.0 %all-reduce.5.cloned.1.call-done = (bf16[3,1024,512]{1,2,0:T(8,128)(2,1)}, bf16[512,1024]{1,0:T(8,128)(2,1)}, bf16[1024,2048]{1,0:T(8,128)(2,1)}, bf16[2048,1024]{1,0:T(8,128)(2,1)}) async-done(((bf16[3,1024,512]{1,2,0:T(8,128)(2,1)}, bf16[512,1024]{1,0:T(8,128)(2,1)}, bf16[1024,2048]{1,0:T(8,128)(2,1)}, bf16[2048,1024]{1,0:T(8,128)(2,1)}), (bf16[3,1024,512]{1,2,0:T(8,128)(2,1)}, ...) | async-done | bytes 12582928 | tf_op jit(solution)/shard_map/psum | solution.py:239
  1504.3 41.2 %reduce-scatter.11.cloned.1.call-done = bf16[1120,1024]{1,0:T(8,128)(2,1)} async-done(((bf16[2240,1024]{1,0:T(8,128)(2,1)}), bf16[1120,1024]{1,0:T(8,128)(2,1)}) %reduce-scatter.11.cloned.1.call-update) | async-done | bytes 2293776 | tf_op jit(solution)/shard_map/reduce_scatter | solution.py:218
  1550.0 40.3 %all-reduce = (f32[4,1024]{1,0:T(4,128)}, f32[4,1024]{1,0:T(4,128)}, f32[2,1024]{1,0:T(2,128)}) all-reduce(f32[4,1024]{1,0:T(4,128)S(1)} %pad_maximum_fusion.5, f32[4,1024]{1,0:T(4,128)S(1)} %pad_maximum_fusion.6, f32[2,1024]{1,0:T(2,128)S(1)} %pad_maximum_fusion.8), channel_id=1, replica_groups=mesh['dp'=16,'mp'=2] {'dp','mp'}, use_global_device_ids=true, to_apply=%region_34.35 | all-reduce | flops 10240 | bytes 81920 | tf_op jit(solution)/shard_map/psum | solution.py:237
  (292 shorter events, 446.8 us)
Async XLA Ops:
  7.2 72.4 %copy-start = (bf16[3,1024,512]{2,1,0:T(8,128)(2,1)S(1)}, bf16[3,1024,512]{2,1,0:T(8,128)(2,1)}, u32[]{:S(2)}) copy-start(bf16[3,1024,512]{2,1,0:T(8,128)(2,1)} %param.22) | copy-start | bytes 9437188
  7.2 72.3 %all-gather.5.cloned.1.call-start = ((), (), s32[]{:S(2)}) async-start(), calls=%async_computation.4 | async-start | bytes 6881280 | tf_op jit(solution)/shard_map/all_gather | solution.py:78
  15.5 385.4 %reduce-scatter.5.cloned.1.call-start = ((), (), s32[]{:S(2)}) async-start(), calls=%async_computation.5 | async-start | bytes 13762560 | tf_op jit(solution)/shard_map/reduce_scatter | solution.py:127
  273.6 11.2 copy-start.15
  293.0 179.6 %all-gather.7.cloned.1.call-start = ((), (), s32[]{:S(2)}) async-start(), calls=%async_computation.6 | async-start | bytes 6881280 | tf_op jit(solution)/shard_map/all_gather | solution.py:139
  409.1 63.5 %copy-start.46 = (f32[2048]{0:T(1024)S(1)}, f32[2048]{0:T(1024)}, u32[]{:S(2)}) copy-start(f32[2048]{0:T(1024)} %param.27) | copy-start | bytes 24580
  411.3 204.9 %reduce-scatter.7.cloned.1.call-start = ((), (), s32[]{:S(2)}) async-start(), calls=%async_computation.7 | async-start | bytes 13762560 | tf_op jit(solution)/shard_map/reduce_scatter | solution.py:143
  472.7 23.6 %copy-start.44 = (bf16[2048,1024]{1,0:T(8,128)(2,1)S(1)}, bf16[2048,1024]{1,0:T(8,128)(2,1)}, u32[]{:S(2)}) copy-start(bf16[2048,1024]{1,0:T(8,128)(2,1)} %param.28) | copy-start | bytes 12582916
  508.4 180.8 %all-gather.9.cloned.1.call-start = ((), (), s32[]{:S(2)}) async-start(), calls=%async_computation.8 | async-start | bytes 6881280 | tf_op jit(solution)/shard_map/all_gather | solution.py:156
  616.3 7.1 slice-start
  627.9 211.5 %reduce-scatter.9.cloned.1.call-start = ((), (), s32[]{:S(2)}) async-start(), calls=%async_computation.9 | async-start | bytes 13762560 | tf_op jit(solution)/shard_map/reduce_scatter | solution.py:163
  689.2 27.8 %copy-start.45 = (bf16[1024,2048]{1,0:T(8,128)(2,1)S(1)}, bf16[1024,2048]{1,0:T(8,128)(2,1)}, u32[]{:S(2)}) copy-start(bf16[1024,2048]{1,0:T(8,128)(2,1)} %param.26) | copy-start | bytes 12582916
  731.5 186.5 %all-gather.11.cloned.1.call-start = ((), (), s32[]{:S(2)}) async-start(), calls=%async_computation.10 | async-start | bytes 6881280 | tf_op jit(solution)/shard_map/all_gather | solution.py:172
  839.4 13.8 slice-start.2
  844.9 8.3 slice-start.3
  856.6 628.0 %all-reduce.5.cloned.1.call-start = ((), (), s32[]{:S(2)}) async-start(), calls=%async_computation.12 | async-start | bytes 25165824 | tf_op jit(solution)/shard_map/psum | solution.py:239
  931.4 8.0 copy-start.16
  985.3 10.6 copy-start.4
  1049.8 10.6 copy-start.4
  1114.3 10.6 copy-start.4
  1178.8 10.5 copy-start.4
  1225.7 14.0 slice-start.4
  1248.9 296.6 %reduce-scatter.11.cloned.1.call-start = ((), (), s32[]{:S(2)}) async-start(), calls=%async_computation.11 | async-start | bytes 6881280 | tf_op jit(solution)/shard_map/reduce_scatter | solution.py:218
  1499.8 45.7 %copy-start.18 = (f32[1120]{0:T(1024)S(1)}, f32[1120]{0:T(1024)}, u32[]{:S(2)}) copy-start(f32[1120]{0:T(1024)} %copy-done.17) | copy-start | bytes 13444
  1499.8 45.7 %copy-start.20 = (f32[1120]{0:T(1024)S(1)}, f32[1120]{0:T(1024)}, u32[]{:S(2)}) copy-start(f32[1120]{0:T(1024)} %copy-done.19) | copy-start | bytes 13444
  1499.8 45.7 %copy-start.22 = (f32[1,1024]{1,0:T(1,128)S(1)}, f32[1,1024]{1,0:T(1,128)}, u32[]{:S(2)}) copy-start(f32[1,1024]{1,0:T(1,128)} %copy-done.21) | copy-start | bytes 12292
  1504.3 45.6 %copy-start.27 = (f32[1024]{0:T(1024)S(1)}, f32[1024]{0:T(1024)}, u32[]{:S(2)}) copy-start(f32[1024]{0:T(1024)} %get-tuple-element.451) | copy-start | bytes 12292
  1504.3 45.6 %copy-start.31 = (f32[1024]{0:T(1024)S(1)}, f32[1024]{0:T(1024)}, u32[]{:S(2)}) copy-start(f32[1024]{0:T(1024)} %get-tuple-element.449) | copy-start | bytes 12292
  1504.3 45.6 %copy-start.37 = (f32[1024]{0:T(1024)S(1)}, f32[1024]{0:T(1024)}, u32[]{:S(2)}) copy-start(f32[1024]{0:T(1024)} %get-tuple-element.453) | copy-start | bytes 12292
  1504.3 45.7 %copy-start.26 = (f32[1024]{0:T(1024)S(1)}, f32[1024]{0:T(1024)}, u32[]{:S(2)}) copy-start(f32[1024]{0:T(1024)} %get-tuple-element.460) | copy-start | bytes 12292
  1504.3 45.7 %copy-start.30 = (f32[1024]{0:T(1024)S(1)}, f32[1024]{0:T(1024)}, u32[]{:S(2)}) copy-start(f32[1024]{0:T(1024)} %get-tuple-element.459) | copy-start | bytes 12292
  1504.3 45.7 %copy-start.36 = (f32[1024]{0:T(1024)S(1)}, f32[1024]{0:T(1024)}, u32[]{:S(2)}) copy-start(f32[1024]{0:T(1024)} %get-tuple-element.464) | copy-start | bytes 12292
  (37 other events, 164.4 us)
Sparse Core Ops, SparseCore 0:
  15.6 63.8 all-gather.4
  293.2 107.7 reduce-scatter.4
  411.4 61.1 all-gather.6
  508.5 107.7 reduce-scatter.6
  628.0 61.1 all-gather.8
  731.6 107.7 reduce-scatter.8
  856.7 61.1 all-gather.10
  1249.0 235.4 all-reduce.4
  1486.9 58.5 reduce-scatter.10
where the time goes:
time: 1610 us; the launch traced here: 1600 us
  waiting for transfers between devices  762 us (47%)
  matrix products  408 us (25%)
  other arithmetic  174 us (11%)
  local copies, waits for them, and re-layouts  144 us (9%)
  blocking collectives  76.4 us (5%)
  loops' own time  21.9 us (1%)
    psum x1, waiting for transfers between devices, shards(): lax.psum(grad_w_qkv.astype(jnp.bfloat16), 'dp').astype(jnp.float32)  182 us
    reduce_scatter x1, waiting for transfers between devices, shards(): lax.psum_scatter(jnp.einsum('tf,df->td', d_up, w_up, preferred_element_ty...  108 us
    reduce_scatter x1, waiting for transfers between devices, shards(): lax.psum_scatter(jnp.dot(activated, w_down, preferred_element_type=jnp.fl...  107 us
    reduce_scatter x1, waiting for transfers between devices, shards(): lax.psum_scatter(jnp.dot(mixed_heads, w_out, preferred_element_type=jnp.f...  107 us
    dot_general x8, matrix products, block_probs(): jnp.einsum('qhd,khd->hqk', query_block, key_seq, preferred_element_type=j...  83.7 us
    all_gather x1, waiting for transfers between devices, shards(): first_all = lax.all_gather(first_in, 'mp', axis=0, tiled=True)  63.3 us
    all_gather x1, waiting for transfers between devices, shards(): d_down_all = lax.all_gather(d_down_low, 'mp', axis=0, tiled=True)  61.3 us
    all_gather x1, waiting for transfers between devices, shards(): third_all = lax.all_gather(third_in, 'mp', axis=0, tiled=True)  61.3 us
  transfers between devices with their start and end apart: 9, of which 9 were waited for; matrix products, arithmetic and copies ran while one was open for 4% of the time, Pallas kernels for 0%

commit v1 on v0

--- a/solution.py
+++ b/solution.py
@@ -4,6 +4,8 @@
 import jax
 import jax.numpy as jnp
 from jax import lax
+from jax.experimental import pallas as pl
+from jax.experimental.pallas import tpu as pltpu
 from jax.sharding import PartitionSpec as P
 
 HD = 64
@@ -258,6 +260,494 @@
     )
 
 
+LOG2E = 1.4426950408889634
+HIDDEN = -1e30
+
+
+def dot_nt(a, b):
+    return lax.dot_general(a, b, (((1,), (1,)), ((), ())), preferred_element_type=jnp.float32)
+
+
+def dot_nn(a, b):
+    return lax.dot_general(a, b, (((1,), (0,)), ((), ())), preferred_element_type=jnp.float32)
+
+
+def dot_tn(a, b):
+    return lax.dot_general(a, b, (((0,), (0,)), ((), ())), preferred_element_type=jnp.float32)
+
+
+def attend_kernel(rows, bias_ref, q_ref, k_ref, v_ref, out_ref, weight_ref, inv_ref):
+    length = q_ref.shape[0]
+    bias = bias_ref[...]
+    lane = lax.broadcasted_iota(jnp.int32, (1, 2 * HD), 1)
+    keys = k_ref[...]
+    values = v_ref[...]
+    for first in range(0, length, rows):
+        part = pl.ds(first, rows)
+        queries = q_ref[part, :]
+        query_places = lax.broadcasted_iota(jnp.int32, (rows, length), 0) + first
+        key_places = lax.broadcasted_iota(jnp.int32, (rows, length), 1)
+        hide = jnp.where(key_places <= query_places, 0.0, bias)
+        outs, invs = [], []
+        for head in range(2):
+            mine = jnp.where((lane // HD) == head, queries, jnp.zeros_like(queries))
+            scores = dot_nt(mine, keys) + hide
+            top = jnp.max(scores, axis=1, keepdims=True)
+            weights = jnp.exp2((scores - top) * (relax_factor * LOG2E))
+            inv = 1.0 / jnp.sum(weights, axis=1, keepdims=True)
+            low = weights.astype(jnp.bfloat16)
+            weight_ref[head, part, :] = low
+            outs.append(dot_nn(low, values) * inv)
+            invs.append(inv)
+        out_ref[part, :] = jnp.where(lane < HD, outs[0], outs[1]).astype(jnp.bfloat16)
+        inv_ref[part, :] = jnp.where(lane < HD, invs[0], invs[1])
+
+
+def attend(queries, keys, values, bias):
+    length, width = queries.shape
+    pairs = width // (2 * HD)
+    column = pl.BlockSpec((length, 2 * HD), lambda i: (0, i))
+    return pl.pallas_call(
+        partial(attend_kernel, length // 2),
+        grid=(pairs,),
+        in_specs=[pl.BlockSpec((1, length), lambda i: (0, 0)), column, column, column],
+        out_specs=[column, pl.BlockSpec((2, length, length), lambda i: (i, 0, 0)), column],
+        out_shape=[
+            jax.ShapeDtypeStruct((length, width), jnp.bfloat16),
+            jax.ShapeDtypeStruct((2 * pairs, length, length), jnp.bfloat16),
+            jax.ShapeDtypeStruct((length, width), jnp.float32),
+        ],
+        compiler_params=pltpu.CompilerParams(vmem_limit_bytes=56 * 2**20),
+        cost_estimate=pl.CostEstimate(
+            flops=pairs * 6 * 10**9, bytes_accessed=pairs * 7 * 10**6, transcendentals=0
+        ),
+    )(bias, queries, keys, values)
+
+
+def attend_back_kernel(
+    query_scale,
+    q_ref,
+    k_ref,
+    v_ref,
+    out_ref,
+    grad_ref,
+    inv_ref,
+    weight_ref,
+    dq_ref,
+    dk_ref,
+    dv_ref,
+    ds_ref,
+):
+    lane = lax.broadcasted_iota(jnp.int32, (1, 2 * HD), 1)
+    keys = k_ref[...]
+    values = v_ref[...]
+    queries = q_ref[...]
+    scaled = grad_ref[...].astype(jnp.float32) * inv_ref[...]
+    mixed = out_ref[...].astype(jnp.float32)
+    low = scaled.astype(jnp.bfloat16)
+    dqs, dks, dvs = [], [], []
+    for head in range(2):
+        mine = (lane // HD) == head
+        grad = jnp.where(mine, scaled * relax_factor, 0.0).astype(jnp.bfloat16)
+        inner = jnp.sum(grad.astype(jnp.float32) * mixed, axis=1, keepdims=True)
+        d_probs = dot_nt(grad, values)
+        ds_ref[...] = (
+            weight_ref[head].astype(jnp.float32) * (d_probs - inner)
+        ).astype(jnp.bfloat16)
+        dqs.append((dot_nn(ds_ref[...], keys) * query_scale).astype(jnp.bfloat16))
+        dks.append(dot_tn(ds_ref[...], queries).astype(jnp.bfloat16))
+        dvs.append(dot_tn(weight_ref[head], low).astype(jnp.bfloat16))
+    dq_ref[...] = jnp.where(lane < HD, dqs[0], dqs[1])
+    dk_ref[...] = jnp.where(lane < HD, dks[0], dks[1])
+    dv_ref[...] = jnp.where(lane < HD, dvs[0], dvs[1])
+
+
+def attend_back(queries, keys, values, mixed, grad, inv, weights, query_scale):
+    length, width = queries.shape
+    pairs = width // (2 * HD)
+    column = pl.BlockSpec((length, 2 * HD), lambda i: (0, i))
+    return pl.pallas_call(
+        partial(attend_back_kernel, query_scale),
+        grid=(pairs,),
+        in_specs=[column] * 6 + [pl.BlockSpec((2, length, length), lambda i: (i, 0, 0))],
+        out_specs=[column] * 3,
+        out_shape=[jax.ShapeDtypeStruct((length, width), jnp.bfloat16)] * 3,
+        scratch_shapes=[pltpu.VMEM((length, length), jnp.bfloat16)],
+        compiler_params=pltpu.CompilerParams(vmem_limit_bytes=56 * 2**20),
+        cost_estimate=pl.CostEstimate(
+            flops=pairs * 7 * 10**9, bytes_accessed=pairs * 7 * 10**6, transcendentals=0
+        ),
+    )(queries, keys, values, mixed, grad, inv, weights)
+
+
+def flip(value, bit):
+    count = lax.axis_size("dp")
+    return lax.ppermute(value, "dp", [(i, i ^ bit) for i in range(count)])
+
+
+def cross(value):
+    return lax.ppermute(value, "mp", [(0, 1), (1, 0)])
+
+
+def block(value, index, count, axis):
+    size = value.shape[axis] // count
+    return lax.dynamic_slice_in_dim(value, index * size, size, axis)
+
+
+def low(value):
+    return value.astype(jnp.bfloat16)
+
+
+MESH = pl.DeviceIdType.MESH
+CHUNK = 128
+
+
+def reduce_kernel(quarters, *refs):
+    count = len(quarters)
+    owns, others = refs[:count], refs[count : 2 * count]
+    (out, mine, core_in, held, x_out, x_in, y_out, y_in, z_out, z_in, last) = refs[2 * count : 2 * count + 11]
+    (load_sem, core_sem, x_sem, y_sem, z_sem, zz_sem, yy_sem, cc_sem, keep_sem) = refs[2 * count + 11 :]
+    place = lax.axis_index("dp")
+    turn = lax.axis_index("mp")
+    core, side, level = place % 2, (place // 2) % 2, place // 4
+    levels = lax.axis_size("dp") // 4
+    sibling = {"dp": place + 1 - 2 * core}
+    across = {"mp": 1 - turn}
+    beside = {"dp": place + 2 - 4 * side}
+    floors = [{"dp": (level + step) % levels * 4 + place % 4} for step in range(1, levels)]
+    half, piece = CHUNK // 2, CHUNK // 2 // levels
+    chunks = sum(quarters) // CHUNK
+
+    barrier = pltpu.get_barrier_semaphore()
+    partners = [sibling, across, beside, *floors]
+    for partner in partners:
+        pl.semaphore_signal(barrier, inc=1, device_id=partner, device_id_type=MESH)
+    pl.semaphore_wait(barrier, len(partners))
+
+    def rows(start, size):
+        return pl.ds(pl.multiple_of(start, 16), size)
+
+    def remote(source, target, sems, index, device):
+        return pltpu.make_async_remote_copy(
+            src_ref=source,
+            dst_ref=target,
+            send_sem=sems.at[(0, *index)],
+            recv_sem=sems.at[(1, *index)],
+            device_id=device,
+            device_id_type=MESH,
+        )
+
+    def loads(weight, offset, slot):
+        copies = []
+        for index, refs_of in enumerate((others, owns)):
+            ref, quarter = refs_of[weight], quarters[weight]
+            copies.append(
+                pltpu.make_async_copy(
+                    ref.at[rows(core * quarter + offset, CHUNK)], mine.at[index], load_sem.at[index]
+                )
+            )
+            copies.append(
+                remote(
+                    ref.at[rows((1 - core) * quarter + offset, CHUNK)],
+                    core_in.at[slot, index],
+                    core_sem,
+                    (slot, index),
+                    sibling,
+                )
+            )
+        return copies
+
+    def x_copy(slot):
+        return remote(x_out, x_in.at[slot], x_sem, (slot,), across)
+
+    def y_copy(slot):
+        return remote(y_out.at[rows((1 - side) * half, half)], y_in.at[slot], y_sem, (slot,), beside)
+
+    def z_copies(slot):
+        return [
+            remote(
+                z_out.at[rows((level + step) % levels * piece, piece)],
+                z_in.at[slot, step - 1],
+                z_sem,
+                (slot, step - 1),
+                floors[step - 1],
+            )
+            for step in range(1, levels)
+        ]
+
+    def keep_copies(chunk, slot):
+        target = out.at[core, rows(chunk * CHUNK + side * half + level * piece, piece)]
+        copies = [pltpu.make_async_copy(last, target, keep_sem)]
+        for step in range(1, levels):
+            copies.append(remote(last, target, zz_sem, (slot, step - 1), floors[step - 1]))
+        return copies
+
+    def yy_copy(chunk, slot):
+        part = out.at[core, rows(chunk * CHUNK + side * half, half)]
+        return remote(part, part, yy_sem, (slot,), beside)
+
+    def cc_copy(chunk, slot):
+        part = out.at[core, rows(chunk * CHUNK, CHUNK)]
+        return remote(part, part, cc_sem, (slot,), sibling)
+
+    def wide(value):
+        return value.astype(jnp.float32)
+
+    def at_stage(turn_now, stage, action):
+        chunk = turn_now - stage
+
+        @pl.when((chunk >= 0) & (chunk < chunks))
+        def _():
+            action(chunk, chunk % 2)
+
+    def stage_7(chunk, slot):
+        cc_copy(chunk, slot).wait()
+
+    def stage_6(chunk, slot):
+        yy_copy(chunk, slot).wait()
+        cc_copy(chunk, slot).start()
+
+    def stage_5(chunk, slot):
+        for copy in keep_copies(chunk, slot):
+            copy.wait()
+        yy_copy(chunk, slot).start()
+
+    def stage_4(chunk, slot):
+        for copy in z_copies(slot):
+            copy.wait()
+        total = wide(z_out[rows(level * piece, piece), :])
+        for step in range(1, levels):
+            total = total + wide(z_in[slot, step - 1])
+        last[...] = low(total)
+        for copy in keep_copies(chunk, slot):
+            copy.start()
+
+    def stage_3(chunk, slot):
+        y_copy(slot).wait()
+        z_out[...] = low(wide(y_out[rows(side * half, half), :]) + wide(y_in[slot]))
+        for copy in z_copies(slot):
+            copy.start()
+
+    def stage_2(chunk, slot):
+        x_copy(slot).wait()
+        y_out[...] = low(held[...] + wide(x_in[slot]))
+        y_copy(slot).start()
+
+    def stage_1(chunk, slot):
+        for copy in loads(0, 0, slot):
+            copy.wait()
+        x_out[...] = low(wide(mine[0]) + wide(core_in[slot, 0]))
+        x_copy(slot).start()
+        held[...] = wide(mine[1]) + wide(core_in[slot, 1])
+
+    def stage_0(chunk, slot):
+        first = 0
+        for weight, quarter in enumerate(quarters):
+            span = quarter // CHUNK
+
+            @pl.when((chunk >= first) & (chunk < first + span))
+            def _(weight=weight, first=first):
+                for copy in loads(weight, (chunk - first) * CHUNK, slot):
+                    copy.start()
+
+            first += span
+
+    stages = [stage_0, stage_1, stage_2, stage_3, stage_4, stage_5, stage_6, stage_7]
+
+    @pl.loop(0, chunks + len(stages) - 1)
+    def _(now):
+        for stage in reversed(range(len(stages))):
+            at_stage(now, stage, stages[stage])
+
+
+def reduce_all(owns, others):
+    width = owns[0].shape[1]
+    quarters = tuple(own.shape[0] // 2 for own in owns)
+    levels = lax.axis_size("dp") // 4
+    half, piece = CHUNK // 2, CHUNK // 2 // levels
+    kind = jnp.bfloat16
+    sem = pltpu.SemaphoreType.DMA
+    return pl.pallas_call(
+        partial(reduce_kernel, quarters),
+        in_specs=[pl.BlockSpec(memory_space=pl.ANY)] * (2 * len(owns)),
+        out_specs=pl.BlockSpec(memory_space=pl.ANY),
+        out_shape=jax.ShapeDtypeStruct((2, sum(quarters), width), kind),
+        scratch_shapes=[
+            pltpu.VMEM((2, CHUNK, width), kind),
+            pltpu.VMEM((2, 2, CHUNK, width), kind),
+            pltpu.VMEM((CHUNK, width), jnp.float32),
+            pltpu.VMEM((CHUNK, width), kind),
+            pltpu.VMEM((2, CHUNK, width), kind),
+            pltpu.VMEM((CHUNK, width), kind),
+            pltpu.VMEM((2, half, width), kind),
+            pltpu.VMEM((half, width), kind),
+            pltpu.VMEM((2, levels - 1, piece, width), kind),
+            pltpu.VMEM((piece, width), kind),
+            sem((2,)),
+            sem((2, 2, 2)),
+            sem((2, 2)),
+            sem((2, 2)),
+            sem((2, 2, levels - 1)),
+            sem((2, 2, levels - 1)),
+            sem((2, 2)),
+            sem((2, 2)),
+            sem,
+        ],
+        compiler_params=pltpu.CompilerParams(collective_id=0, has_side_effects=True, vmem_limit_bytes=56 * 2**20),
+    )(*owns, *others)
+
+
+def sequence_shards(
+    tokens,
+    cond_flags,
+    seg_lengths,
+    norm_gains,
+    norm_biases,
+    w_qkv,
+    qv_bias,
+    w_out,
+    out_biases,
+    w_up,
+    up_bias,
+    w_down,
+    cotangent,
+):
+    length = tokens.shape[0]
+    place = lax.axis_index("dp")
+    turn = lax.axis_index("mp")
+    core = place % 2
+    side = (place // 2) % 2
+    query_scale = 1.0 / (relax_factor * math.sqrt(HD))
+
+    def in_order(which, mine, other, axis):
+        return jnp.where(
+            which == 0,
+            jnp.concatenate([mine, other], axis=axis),
+            jnp.concatenate([other, mine], axis=axis),
+        )
+
+    def fetch(weight, axis):
+        first = cross(block(weight, 2 * core + side, 4, axis))
+        near = in_order(side, first, flip(first, 2), axis)
+        return in_order(core, near, flip(near, 1), axis)
+
+    qkv_sets = (w_qkv, fetch(w_qkv, 2))
+    bias_sets = (qv_bias, cross(qv_bias))
+    out_sets = (w_out, fetch(w_out, 0))
+    up_sets = (w_up, fetch(w_up, 1))
+    up_bias_sets = (up_bias, cross(up_bias))
+    down_sets = (w_down, fetch(w_down, 0))
+
+    marks = token_marks(
+        lax.dynamic_index_in_dim(cond_flags, turn, 0, keepdims=False),
+        lax.dynamic_index_in_dim(seg_lengths, turn, 0, keepdims=False),
+        length,
+    )
+    hide = jnp.where(marks[None, :] == 1, 0.0, HIDDEN).astype(jnp.float32)
+
+    source = tokens.astype(jnp.float32)
+    normed_one, scale_one = standardize(source)
+    first_in = low(normed_one * norm_gains[0] + norm_biases[0])
+    heads = []
+    attended = out_biases[0]
+    for weight, bias, out in zip(qkv_sets, bias_sets, out_sets):
+        queries = low((dot_nn(first_in, weight[0]) + bias[0]) * query_scale)
+        keys = low(dot_nn(first_in, weight[1]))
+        values = low(dot_nn(first_in, weight[2]) + bias[1])
+        mixed, kept, inv = attend(queries, keys, values, hide)
+        heads.append((queries, keys, values, mixed, kept, inv))
+    for (_, _, _, mixed, _, _), out in zip(heads, out_sets):
+        attended = attended + dot_nn(mixed, out)
+    normed_two, scale_two = standardize(attended)
+    residual = source + normed_two * norm_gains[1] + norm_biases[1]
+    normed_three, scale_three = standardize(residual)
+    third_in = low(normed_three * norm_gains[2] + norm_biases[2])
+    ups = [dot_nn(third_in, weight) + bias for weight, bias in zip(up_sets, up_bias_sets)]
+    acts = [low(jax.nn.gelu(up, approximate=True)) for up in ups]
+    down = out_biases[1]
+    for act, weight in zip(acts, down_sets):
+        down = down + dot_nn(act, weight)
+    normed_four, scale_four = standardize(down)
+    result = low(residual + normed_four * norm_gains[3] + norm_biases[3])
+    grad_out = cotangent.astype(jnp.float32)
+    d_down = norm_back(grad_out, normed_four, scale_four, norm_gains[3])
+    d_down_low = low(d_down)
+
+    d_ups = []
+    for up, weight in zip(ups, down_sets):
+        pull = jax.vjp(partial(jax.nn.gelu, approximate=True), up)[1]
+        d_ups.append(low(pull(dot_nt(d_down_low, weight))[0]))
+
+    down_parts = [low(dot_tn(act, d_down_low)) for act in acts]
+    up_parts = [low(dot_tn(grad, third_in)) for grad in d_ups]
+    d_third = sum(dot_nt(grad, weight) for grad, weight in zip(d_ups, up_sets))
+    d_residual = grad_out + norm_back(d_third, normed_three, scale_three, norm_gains[2])
+    d_attended = norm_back(d_residual, normed_two, scale_two, norm_gains[1])
+    d_att_low = low(d_attended)
+    out_parts = [low(dot_tn(item[3], d_att_low)) for item in heads]
+    d_qkvs = []
+    d_first = 0.0
+    for item, weight, out in zip(heads, qkv_sets, out_sets):
+        queries, keys, values, mixed, kept, inv = item
+        d_mixed = low(dot_nt(d_att_low, out))
+        grads = attend_back(queries, keys, values, mixed, d_mixed, inv, kept, query_scale)
+        d_qkvs.append(grads)
+        for index in range(3):
+            d_first = d_first + dot_nt(grads[index], weight[index])
+
+    qkv_parts = [[low(dot_tn(grads[index], first_in)) for grads in d_qkvs] for index in range(3)]
+    parts = [down_parts, up_parts, out_parts, *qkv_parts]
+    total = reduce_all([part[0] for part in parts], [part[1] for part in parts])
+    spans = [0]
+    for part in parts:
+        spans.append(spans[-1] + part[0].shape[0] // 2)
+    wholes = [
+        total[:, first:last].reshape(-1, total.shape[2]).astype(jnp.float32)
+        for first, last in zip(spans[:-1], spans[1:])
+    ]
+    grad_w_down, grad_w_up, grad_w_out = wholes[0], wholes[1].T, wholes[2]
+    grad_w_qkv = jnp.stack([whole.T for whole in wholes[3:]])
+    grad_input = d_residual + norm_back(d_first, normed_one, scale_one, norm_gains[0])
+
+    error_terms = (d_first, d_residual, d_third, grad_out)
+    normed_terms = (normed_one, normed_two, normed_three, normed_four)
+    sums = jnp.stack(
+        [jnp.sum(error * normed, axis=0) for error, normed in zip(error_terms, normed_terms)]
+        + [jnp.sum(error, axis=0) for error in error_terms]
+        + [jnp.sum(d_attended, axis=0), jnp.sum(d_down, axis=0)]
+    )
+
+    def columns(value):
+        return jnp.sum(value, axis=0, dtype=jnp.float32)
+
+    qv_sums = [jnp.stack([columns(grads[0]), columns(grads[2])]) for grads in d_qkvs]
+    up_sums = [columns(grad) for grad in d_ups]
+    own_small = jnp.concatenate([qv_sums[0].reshape(-1), up_sums[0]])
+    other_small = jnp.concatenate([qv_sums[1].reshape(-1), up_sums[1]])
+    small = jnp.concatenate([sums.reshape(-1), own_small])
+    small = small + cross(jnp.concatenate([sums.reshape(-1), other_small]))
+    bit = 1
+    while bit < lax.axis_size("dp"):
+        small = small + flip(small, bit)
+        bit *= 2
+    sums = small[: sums.size].reshape(sums.shape)
+    grad_qv_bias = small[sums.size : sums.size + qv_bias.size].reshape(qv_bias.shape)
+    grad_up_bias = small[sums.size + qv_bias.size :]
+    return (
+        result,
+        grad_input,
+        sums[:4],
+        sums[4:8],
+        grad_w_qkv,
+        grad_qv_bias,
+        grad_w_out,
+        sums[8:],
+        grad_w_up,
+        grad_up_bias,
+        grad_w_down,
+    )
+
+
 def solution(mesh):
     in_specs = (
         P(("dp", "mp"), None),
@@ -287,4 +777,13 @@
         P("mp"),
         P("mp", None),
     )
-    return jax.shard_map(shards, mesh=mesh, in_specs=in_specs, out_specs=out_specs, check_vma=False)
+    per_device = mesh.shape["dp"] * mesh.shape["mp"]
+
+    def step(*args):
+        whole_sequences = args[1].shape[0] == per_device
+        local = sequence_shards if whole_sequences and mesh.shape["mp"] == 2 and mesh.shape["dp"] == 16 else shards
+        return jax.shard_map(
+            local, mesh=mesh, in_specs=in_specs, out_specs=out_specs, check_vma=False
+        )(*args)
+
+    return step

time: 1610 us -> 681 us (0.42)
  waiting for transfers between devices: 762 us -> 68 us
  Pallas kernels: 0 us -> 289 us
  matrix products: 408 us -> 193 us
  other arithmetic: 174 us -> 62.2 us
  local copies, waits for them, and re-layouts: 144 us -> 40.5 us
  blocking collectives: 76.4 us -> 0 us
  loops' own time: 21.9 us -> 0 us
  starting transfers between devices: 0.96 us -> 19.6 us
    reduce_scatter x4 -> x0, waiting for transfers between devices: 364 us -> none  [the longest x1 108 us: shards(): lax.psum_scatter(jnp.einsum('tf,df->td', d_up, w_up, preferred_element_ty...]
    pallas_call x0 -> x5, Pallas kernels: none -> 289 us  [the longest x1 191 us: reduce_all(): pl.pallas_call(partial(reduce_kernel, quarters), in_specs=[pl.BlockSpec(m...]
    all_gather x4 -> x0, waiting for transfers between devices: 217 us -> none  [the longest x1 63.3 us: shards(): first_all = lax.all_gather(first_in, 'mp', axis=0, tiled=True)]
    dot_general x40 -> x36, matrix products: 408 us -> 193 us  [the longest x12 67.4 us: dot_nn(): lax.dot_general(a, b, (((1,), (0,)), ((), ())), preferred_element_type=jn...]
    psum x1 -> x0, waiting for transfers between devices: 182 us -> none  [shards(): lax.psum(grad_w_qkv.astype(jnp.bfloat16), 'dp').astype(jnp.float32)]
    psum x2 -> x0, blocking collectives: 76.4 us -> none  [the longest x1 40.3 us: shards(): lax.psum((gain_sums, bias_sums, outer_sums), ('dp', 'mp'))]
    convert_element_type x12 -> x4, other arithmetic: 78.8 us -> 8.03 us  [the longest x2 6.37 us: sequence_shards(): total[:, first:last].reshape(-1, total.shape[2]).astype(jnp.float32)]
    ppermute x0 -> x19, waiting for transfers between devices: none -> 68 us  [the longest x7 44.8 us: cross(): return lax.ppermute(value, 'mp', [(0, 1), (1, 0)])]
  transfers between devices with their start and end apart: 9 -> 19, of which waited for: 9 -> 3; matrix products, arithmetic and copies ran while one was open for 4% -> 19% of each run, Pallas kernels for 0% -> 35%
where the time goes in v1:
time: 681 us; the launch traced here: 675 us
  Pallas kernels  289 us (42%)
  matrix products  193 us (28%)
  waiting for transfers between devices  68 us (10%)
  other arithmetic  62.2 us (9%)
  local copies, waits for them, and re-layouts  40.5 us (6%)
  starting transfers between devices  19.6 us (3%)
    pallas_call x1, Pallas kernels, reduce_all(): pl.pallas_call(partial(reduce_kernel, quarters), in_specs=[pl.BlockSpec(m...  191 us
    dot_general x12, matrix products, dot_nn(): lax.dot_general(a, b, (((1,), (0,)), ((), ())), preferred_element_type=jn...  67.4 us
    dot_general x12, matrix products, dot_nt(): lax.dot_general(a, b, (((1,), (1,)), ((), ())), preferred_element_type=jn...  66.5 us
    dot_general x12, matrix products, dot_tn(): lax.dot_general(a, b, (((0,), (0,)), ((), ())), preferred_element_type=jn...  58.9 us
    pallas_call x2, Pallas kernels, attend_back(): pl.pallas_call(partial(attend_back_kernel, query_scale), grid=(pairs,), i...  53.6 us
    ppermute x7, waiting for transfers between devices, cross(): return lax.ppermute(value, 'mp', [(0, 1), (1, 0)])  44.8 us
    pallas_call x2, Pallas kernels, attend(): pl.pallas_call(partial(attend_kernel, length // 2), grid=(pairs,), in_spe...  44.8 us
    ppermute x12, waiting for transfers between devices, flip(): return lax.ppermute(value, 'dp', [(i, i ^ bit) for i in range(count)])  23.2 us
  transfers between devices with their start and end apart: 19, of which 3 were waited for; matrix products, arithmetic and copies ran while one was open for 19% of the time, Pallas kernels for 35%

profile of v1, /device:TPU:0, one launch (start us, length us, event | category | flops | bytes accessed | tf_op | source)
XLA Modules:
  0.0 675.3 jit_solution(7956146591032181276)
XLA Ops:
  23.2 7.6 %collective-permute-done = bf16[3,1024,128]{2,1,0:T(8,128)(2,1)} collective-permute-done((bf16[3,1024,128]{2,1,0:T(8,128)(2,1)}, bf16[3,1024,128]{2,1,0:T(8,128)(2,1)}, u32[]{:S(2)}, u32[]{:S(2)}) %collective-permute-start) | collective-permute-done | bytes 786464 | tf_op jit(solution)/shard_map/ppermute | solution.py:389
  37.1 37.2 %collective-permute-done.7 = bf16[1024,512]{1,0:T(8,128)(2,1)} collective-permute-done((bf16[1024,512]{1,0:T(8,128)(2,1)}, bf16[1024,512]{1,0:T(8,128)(2,1)}, u32[]{:S(2)}, u32[]{:S(2)}) %collective-permute-start.7) | collective-permute-done | bytes 1048608 | tf_op jit(solution)/shard_map/ppermute | solution.py:389
  78.8 22.3 %shard_map.212 = (bf16[1120,512]{1,0:T(8,128)(2,1)}, bf16[8,1120,1120]{2,1,0:T(8,128)(2,1)}, f32[1120,512]{1,0:T(8,128)}) custom-call(f32[1,1120]{1,0:T(1,128)} %select_n.96.bias_ref, bf16[1120,512]{1,0:T(8,128)(2,1)} %fusion.37.q_ref, bf16[1120,512]{1,0:T(8,128)(2,1)} %convolution_convert_fusion.7.k_ref, bf16[1120,512]{1,0:T(8,128)(2,1)} %fusion.38.v_ref), custom_call_target="tpu_custom_call" | custom-call | flops 24000000000 | bytes 28000000 | tf_op jit(solution)/shard_map/pallas_call | solution.py:310
  103.3 4.8 convolution_add_fusion.8
  109.5 23.2 %collective-permute-done.5 = bf16[128,1024]{1,0:T(8,128)(2,1)} collective-permute-done((bf16[128,1024]{1,0:T(8,128)(2,1)}, bf16[128,1024]{1,0:T(8,128)(2,1)}, u32[]{:S(2)}, u32[]{:S(2)}) %collective-permute-start.5) | collective-permute-done | bytes 262176 | tf_op jit(solution)/shard_map/ppermute | solution.py:385
  134.9 4.4 maximum_select_fusion.3
  139.8 4.6 maximum_select_fusion.4
  154.9 22.5 %shard_map.213 = (bf16[1120,512]{1,0:T(8,128)(2,1)}, bf16[8,1120,1120]{2,1,0:T(8,128)(2,1)}, f32[1120,512]{1,0:T(8,128)}) custom-call(f32[1,1120]{1,0:T(1,128)} %select_n.96.bias_ref, bf16[1120,512]{1,0:T(8,128)(2,1)} %multiply_convert_fusion.2.q_ref, bf16[1120,512]{1,0:T(8,128)(2,1)} %convolution_convert_fusion.6.k_ref, ...), custom_call_target="tpu_custom_call" | custom-call | flops 24000000000 | bytes 28000000 | tf_op jit(solution)/shard_map/pallas_call | solution.py:310
  188.4 7.3 %convolution_add_fusion.1 = f32[1120,2048]{1,0:T(8,128)} fusion(bf16[1120,1024]{1,0:T(8,128)(2,1)S(1)} %add_convert_fusion.1, bf16[1024,2048]{1,0:T(8,128)(2,1)S(1)} %copy-done.30, f32[2048]{0:T(1024)S(1)} %copy-done.58), kind=kOutput, calls=%fused_computation.23 | convolution fusion | flops 4699914240 | bytes 15671296 | tf_op jit(solution)/shard_map/dot_general | solution.py:272
  195.7 11.5 %fusion.65 = f32[1120,1024]{1,0:T(8,128)} fusion(bf16[2048,1024]{1,0:T(8,128)(2,1)S(1)} %copy-done.28, f32[1120,2048]{1,0:T(8,128)} %convolution_add_fusion.1), kind=kOutput, calls=%fused_computation.178 | convolution fusion | flops 4718264320 | bytes 17956864 | tf_op jit(solution)/shard_map/dot_general | solution.py:272
  207.2 12.1 %convolution_add_fusion = f32[1120,2048]{1,0:T(8,128)} fusion(bf16[1120,1024]{1,0:T(8,128)(2,1)S(1)} %add_convert_fusion.1, f32[2048]{0:T(1024)S(1)} %collective-permute-done.10, bf16[1024,1024]{1,0:T(8,128)(2,1)} %collective-permute-done.9, bf16[1024,1024]{1,0:T(8,128)(2,1)} %maximum_select_fusion.3, pred[]{:T(512)S(6)} %eq.48), kind=kOutput, calls=%fused_computation.22 | convolution fusion | flops 4718788608 | bytes 15671297 | tf_op jit(solution)/shard_map/dot_general | solution.py:272
  219.3 14.1 %fusion.83 = (f32[1120]{0:T(1024)S(1)}, f32[1120,1024]{1,0:T(8,128)S(1)}) fusion(bf16[1024,1024]{1,0:T(8,128)(2,1)} %collective-permute-done.13, bf16[1024,1024]{1,0:T(8,128)(2,1)} %maximum_select_fusion.4, pred[]{:T(512)S(6)} %eq.48, f32[1120,2048]{1,0:T(8,128)} %convolution_add_fusion, f32[1120,1024]{1,0:T(8,128)} %fusion.65, f32[1024]{0:T(1024)S(1)} %bitcast.181), kind=kOutput, calls=%fused_computation.193 | convolution fusion | flops 4740578304 | bytes 22552960 | tf_op jit(solution)/shard_map/dot_general | solution.py:272
  241.5 8.1 %convolution_convert_fusion.1.refs_6_ = bf16[2048,1024]{1,0:T(8,128)(2,1)} fusion(bf16[1120,1024]{1,0:T(8,128)(2,1)S(1)} %get-tuple-element.54, f32[1120,2048]{1,0:T(8,128)S(1)} %bitcast.192), kind=kOutput, calls=%fused_computation.83 | convolution fusion | flops 4720361472 | bytes 15663104 | tf_op jit(solution)/shard_map/dot_general | solution.py:276
  249.6 10.9 %convolution_convert_fusion.3.refs_0_ = bf16[2048,1024]{1,0:T(8,128)(2,1)} fusion(bf16[1120,1024]{1,0:T(8,128)(2,1)S(1)} %get-tuple-element.54, f32[1120,2048]{1,0:T(8,128)} %convolution_add_fusion.1), kind=kOutput, calls=%fused_computation.85 | convolution fusion | flops 4720361472 | bytes 15663104 | tf_op jit(solution)/shard_map/dot_general | solution.py:276
  260.5 13.3 %convert_reduce_fusion.1 = (f32[2048]{0:T(1024)}, bf16[1120,2048]{1,0:T(8,128)(2,1)S(1)}) fusion(f32[1120,2048]{1,0:T(8,128)} %convolution_add_fusion.1, bf16[1120,1024]{1,0:T(8,128)(2,1)S(1)} %get-tuple-element.54, bf16[2048,1024]{1,0:T(8,128)(2,1)S(1)} %copy-done.29), kind=kOutput, calls=%fused_computation.19 | convolution fusion | flops 4748081152 | bytes 20258816 | tf_op jit(solution)/shard_map/dot_general | solution.py:268
  273.8 7.3 %convolution_convert_fusion.2.refs_1_ = bf16[2048,1024]{1,0:T(8,128)(2,1)} fusion(bf16[1120,2048]{1,0:T(8,128)(2,1)S(1)} %get-tuple-element.52, bf16[1120,1024]{1,0:T(8,128)(2,1)S(1)} %copy-done.24), kind=kOutput, calls=%fused_computation.84 | convolution fusion | flops 4699717632 | bytes 11075584 | tf_op jit(solution)/shard_map/dot_general | solution.py:276
  281.0 6.6 fusion.84
  287.6 16.7 %convert_reduce_fusion = (f32[2048]{0:T(1024)S(1)}, bf16[1120,2048]{1,0:T(8,128)(2,1)}) fusion(f32[1120,2048]{1,0:T(8,128)} %convolution_add_fusion, bf16[1120,1024]{1,0:T(8,128)(2,1)S(1)} %copy-done.26, bf16[1024,1024]{1,0:T(8,128)(2,1)} %collective-permute-done.13, bf16[1024,1024]{1,0:T(8,128)(2,1)} %maximum_select_fusion.4, pred[]{:T(512)S(6)} %eq.48), kind=kOutput, calls=%fused_computation.18 | convolution fusion | flops 4766955520 | bytes 20258816 | tf_op jit(solution)/shard_map/dot_general | solution.py:268
  304.3 9.8 %convolution_convert_fusion.refs_7_ = bf16[2048,1024]{1,0:T(8,128)(2,1)} fusion(bf16[1120,2048]{1,0:T(8,128)(2,1)} %get-tuple-element.94, bf16[1120,1024]{1,0:T(8,128)(2,1)} %copy-done.23), kind=kOutput, calls=%fused_computation.82 | convolution fusion | flops 4699717632 | bytes 11075584 | tf_op jit(solution)/shard_map/dot_general | solution.py:276
  314.1 12.2 %multiply_reduce_fusion = (f32[1024]{0:T(1024)S(1)}, f32[1120]{0:T(1024)S(1)}, f32[1120]{0:T(1024)S(1)}, f32[1024]{0:T(1024)S(1)}, f32[1120,1024]{1,0:T(8,128)}) fusion(f32[1120,1024]{1,0:T(8,128)S(1)} %get-tuple-element.59, f32[1120]{0:T(1024)S(1)} %copy-done.43, f32[1120]{0:T(1024)S(1)} %copy-done.37, f32[1024]{0:T(1024)S(1)} %bitcast.161, ...), kind=kOutput, calls=%fused_computation.60 | convolution fusion | flops 4727959552 | bytes 22574592 | tf_op jit(solution)/shard_map/dot_general | solution.py:268
  326.4 6.1 multiply_reduce_fusion.1
  341.2 27.0 %shard_map.215 = (bf16[1120,512]{1,0:T(8,128)(2,1)}, bf16[1120,512]{1,0:T(8,128)(2,1)}, bf16[1120,512]{1,0:T(8,128)(2,1)}) custom-call(bf16[1120,512]{1,0:T(8,128)(2,1)} %multiply_convert_fusion.2.q_ref, bf16[1120,512]{1,0:T(8,128)(2,1)} %convolution_convert_fusion.6.k_ref, bf16[1120,512]{1,0:T(8,128)(2,1)} %add_convert_fusion.2.v_ref, ...), custom_call_target="tpu_custom_call" | custom-call | flops 28000000000 | bytes 28000000 | tf_op jit(solution)/shard_map/pallas_call | solution.py:369
  381.3 26.6 %shard_map.214 = (bf16[1120,512]{1,0:T(8,128)(2,1)}, bf16[1120,512]{1,0:T(8,128)(2,1)}, bf16[1120,512]{1,0:T(8,128)(2,1)}) custom-call(bf16[1120,512]{1,0:T(8,128)(2,1)} %fusion.37.q_ref, bf16[1120,512]{1,0:T(8,128)(2,1)} %convolution_convert_fusion.7.k_ref, bf16[1120,512]{1,0:T(8,128)(2,1)} %fusion.38.v_ref, bf16[1120,512]{1,0:T(8,128)(2,1)} %get-tuple-element.23.out_ref, ...), custom_call_target="tpu_custom_call" | custom-call | flops 28000000000 | bytes 28000000 | tf_op jit(solution)/shard_map/pallas_call | solution.py:369
  429.7 4.3 fusion.29
  435.6 190.6 %shard_map.216 = bf16[2,3072,1024]{2,1,0:T(8,128)(2,1)} custom-call(bf16[2048,1024]{1,0:T(8,128)(2,1)} %convolution_convert_fusion.3.refs_0_, bf16[2048,1024]{1,0:T(8,128)(2,1)} %convolution_convert_fusion.2.refs_1_, bf16[512,1024]{1,0:T(8,128)(2,1)} %convolution_convert_fusion.15.refs_2_, bf16[512,1024]{1,0:T(8,128)(2,1)} %convolution_convert_fusion.14.refs_3_, ...), custom_call_target="tpu_custom_call" | custom-call | tf_op jit(solution)/shard_map/pallas_call | solution.py:570
  626.2 4.1 fusion.72
  630.4 4.7 bitcast_convert_fusion
  635.1 4.7 fusion.28
  640.3 4.5 bitcast_convert_fusion.1
  646.1 4.1 fusion.73
  658.5 4.4 maximum_convert_fusion
  662.9 9.1 %copy.31 = f32[2048,1024]{0,1:T(8,128)} copy(f32[2048,1024]{1,0:T(8,128)} %bitcast_convert_fusion.1) | data formatting | bytes 16777216 | tf_op jit(solution)/shard_map/transpose | solution.py:708
  (268 shorter events, 125.6 us)
Async XLA Ops:
  0.7 14.4 %copy-start.59 = (s32[2,3]{1,0:T(2,128)S(1)}, s32[2,3]{1,0:T(2,128)}, u32[]{:S(2)}) copy-start(s32[2,3]{1,0:T(2,128)} %param.14) | copy-start | bytes 76
  0.7 14.4 %copy-start.60 = (s32[2,3]{1,0:T(2,128)S(1)}, s32[2,3]{1,0:T(2,128)}, u32[]{:S(2)}) copy-start(s32[2,3]{1,0:T(2,128)} %param.15) | copy-start | bytes 76
  0.7 17.1 %copy-start.4 = (bf16[1120,1024]{1,0:T(8,128)(2,1)S(1)}, bf16[1120,1024]{1,0:T(8,128)(2,1)}, u32[]{:S(2)}) copy-start(bf16[1120,1024]{1,0:T(8,128)(2,1)} %param.13) | copy-start | bytes 6881284
  0.7 107.4 %collective-permute-start.3 = (f32[2,512]{1,0:T(2,128)}, f32[2,512]{1,0:T(2,128)S(1)}, u32[]{:S(2)}, u32[]{:S(2)}) collective-permute-start(f32[2,512]{1,0:T(2,128)} %param.19), channel_id=1, source_target_pairs={{0,1},{1,0},{2,3},{3,2},{4,5},{5,4},{6,7},{7,6},{8,9},{9,8},{10,11... | collective-permute-start | bytes 12296 | tf_op jit(solution)/shard_map/ppermute | solution.py:389
  4.4 97.3 %collective-permute-start.4 = (bf16[128,1024]{1,0:T(8,128)(2,1)}, bf16[128,1024]{1,0:T(8,128)(2,1)}, u32[]{:S(2)}, u32[]{:S(2)}) collective-permute-start(bf16[128,1024]{1,0:T(8,128)(2,1)} %constant_dynamic-slice_fusion.1), channel_id=1, source_target_pairs={{0,1},{1,0},{2,3},{3,2},{4,5},{5,4},{6,7},{7,6},{8,9},{9,8},{10,11... | collective-permute-start | bytes 786440 | tf_op jit(solution)/shard_map/ppermute | solution.py:389
  7.6 23.2 %collective-permute-start = (bf16[3,1024,128]{2,1,0:T(8,128)(2,1)}, bf16[3,1024,128]{2,1,0:T(8,128)(2,1)}, u32[]{:S(2)}, u32[]{:S(2)}) collective-permute-start(bf16[3,1024,128]{2,1,0:T(8,128)(2,1)} %constant_dynamic-slice_fusion.2), channel_id=1, source_target_pairs={{0,1},{1,0},{2,3},{3,2},{4,5},{5,4},{6,7},{7,6},{8,9},{9,8},{10,11... | collective-permute-start | bytes 2359304 | tf_op jit(solution)/shard_map/ppermute | solution.py:389
  10.8 90.3 %collective-permute-start.11 = (bf16[512,1024]{1,0:T(8,128)(2,1)}, bf16[512,1024]{1,0:T(8,128)(2,1)}, u32[]{:S(2)}, u32[]{:S(2)}) collective-permute-start(bf16[512,1024]{1,0:T(8,128)(2,1)} %constant_dynamic-slice_fusion.3), channel_id=1, source_target_pairs={{0,1},{1,0},{2,3},{3,2},{4,5},{5,4},{6,7},{7,6},{8,9},{9,8},{10,11... | collective-permute-start | bytes 3145736 | tf_op jit(solution)/shard_map/ppermute | solution.py:389
  14.2 60.1 %collective-permute-start.7 = (bf16[1024,512]{1,0:T(8,128)(2,1)}, bf16[1024,512]{1,0:T(8,128)(2,1)}, u32[]{:S(2)}, u32[]{:S(2)}) collective-permute-start(bf16[1024,512]{1,0:T(8,128)(2,1)} %constant_dynamic-slice_fusion), channel_id=1, source_target_pairs={{0,1},{1,0},{2,3},{3,2},{4,5},{5,4},{6,7},{7,6},{8,9},{9,8},{10,11... | collective-permute-start | bytes 3145736 | tf_op jit(solution)/shard_map/ppermute | solution.py:389
  19.1 162.4 %copy-start.44 = (f32[1,1024]{1,0:T(1,128)}, f32[1,1024]{1,0:T(1,128)S(1)}, u32[]{:S(2)}) copy-start(f32[1,1024]{1,0:T(1,128)S(1)} %get-tuple-element.72) | copy-start | bytes 12292
  19.1 167.2 %copy-start.48 = (f32[1,1024]{1,0:T(1,128)}, f32[1,1024]{1,0:T(1,128)S(1)}, u32[]{:S(2)}) copy-start(f32[1,1024]{1,0:T(1,128)S(1)} %get-tuple-element.74) | copy-start | bytes 12292
  20.1 132.4 %copy-start.2 = (bf16[1120,1024]{1,0:T(8,128)(2,1)}, bf16[1120,1024]{1,0:T(8,128)(2,1)S(1)}, u32[]{:S(2)}) copy-start(bf16[1120,1024]{1,0:T(8,128)(2,1)S(1)} %fusion.24) | copy-start | bytes 6881284
  30.8 45.0 %collective-permute-start.1 = (bf16[3,1024,128]{2,1,0:T(8,128)(2,1)}, bf16[3,1024,128]{2,1,0:T(8,128)(2,1)S(1)}, u32[]{:S(2)}, u32[]{:S(2)}) collective-permute-start(bf16[3,1024,128]{2,1,0:T(8,128)(2,1)} %collective-permute-done), channel_id=1, source_target_pairs={{0,4},{2,6},{4,0},{6,2},{8,12},{10,14},{12,8},{14,10},{16,20},{18,... | collective-permute-start | bytes 2359304 | tf_op jit(solution)/shard_map/ppermute | solution.py:385
  74.3 60.6 %collective-permute-start.8 = (bf16[1024,512]{1,0:T(8,128)(2,1)}, bf16[1024,512]{1,0:T(8,128)(2,1)}, u32[]{:S(2)}, u32[]{:S(2)}) collective-permute-start(bf16[1024,512]{1,0:T(8,128)(2,1)} %collective-permute-done.7), channel_id=1, source_target_pairs={{0,4},{2,6},{4,0},{6,2},{8,12},{10,14},{12,8},{14,10},{16,20},{18,... | collective-permute-start | bytes 3145736 | tf_op jit(solution)/shard_map/ppermute | solution.py:385
  78.8 22.9 %copy-start.56 = (f32[2,1024]{1,0:T(2,128)S(1)}, f32[2,1024]{1,0:T(2,128)}, u32[]{:S(2)}) copy-start(f32[2,1024]{1,0:T(2,128)} %param.21) | copy-start | bytes 24580
  78.8 65.6 %collective-permute-start.2 = (bf16[3,1024,256]{2,1,0:T(8,128)(2,1)}, bf16[3,1024,256]{2,1,0:T(8,128)(2,1)}, u32[]{:S(2)}, u32[]{:S(2)}) collective-permute-start(bf16[3,1024,256]{2,1,0:T(8,128)(2,1)} %maximum_select_fusion.5), channel_id=1, source_target_pairs={{0,2},{2,0},{4,6},{6,4},{8,10},{10,8},{12,14},{14,12},{16,18},{18,... | collective-permute-start | bytes 4718600 | tf_op jit(solution)/shard_map/ppermute | solution.py:385
  101.1 38.6 %collective-permute-start.12 = (bf16[512,1024]{1,0:T(8,128)(2,1)}, bf16[512,1024]{1,0:T(8,128)(2,1)}, u32[]{:S(2)}, u32[]{:S(2)}) collective-permute-start(bf16[512,1024]{1,0:T(8,128)(2,1)} %collective-permute-done.11), channel_id=1, source_target_pairs={{0,4},{2,6},{4,0},{6,2},{8,12},{10,14},{12,8},{14,10},{16,20},{18,... | collective-permute-start | bytes 3145736 | tf_op jit(solution)/shard_map/ppermute | solution.py:385
  101.7 31.0 %collective-permute-start.5 = (bf16[128,1024]{1,0:T(8,128)(2,1)}, bf16[128,1024]{1,0:T(8,128)(2,1)}, u32[]{:S(2)}, u32[]{:S(2)}) collective-permute-start(bf16[128,1024]{1,0:T(8,128)(2,1)} %collective-permute-done.4), channel_id=1, source_target_pairs={{0,4},{2,6},{4,0},{6,2},{8,12},{10,14},{12,8},{14,10},{16,20},{18,... | collective-permute-start | bytes 786440 | tf_op jit(solution)/shard_map/ppermute | solution.py:385
  108.1 99.1 %collective-permute-start.10 = (f32[2048]{0:T(1024)S(1)}, f32[2048]{0:T(1024)S(1)}, u32[]{:S(2)}, u32[]{:S(2)}) collective-permute-start(f32[2048]{0:T(1024)S(1)} %copy-done.58), channel_id=1, source_target_pairs={{0,1},{1,0},{2,3},{3,2},{4,5},{5,4},{6,7},{7,6},{8,9},{9,8},{10,11... | collective-permute-start | bytes 24584 | tf_op jit(solution)/shard_map/ppermute | solution.py:389
  134.9 42.5 %collective-permute-start.6 = (bf16[256,1024]{1,0:T(8,128)(2,1)}, bf16[256,1024]{1,0:T(8,128)(2,1)}, u32[]{:S(2)}, u32[]{:S(2)}) collective-permute-start(bf16[256,1024]{1,0:T(8,128)(2,1)} %maximum_select_fusion.13), channel_id=1, source_target_pairs={{0,2},{2,0},{4,6},{6,4},{8,10},{10,8},{12,14},{14,12},{16,18},{18,... | collective-permute-start | bytes 1572872 | tf_op jit(solution)/shard_map/ppermute | solution.py:385
  139.3 67.9 %collective-permute-start.9 = (bf16[1024,1024]{1,0:T(8,128)(2,1)}, bf16[1024,1024]{1,0:T(8,128)(2,1)}, u32[]{:S(2)}, u32[]{:S(2)}) collective-permute-start(bf16[1024,1024]{1,0:T(8,128)(2,1)} %maximum_select_fusion.3), channel_id=1, source_target_pairs={{0,2},{2,0},{4,6},{6,4},{8,10},{10,8},{12,14},{14,12},{16,18},{18,... | collective-permute-start | bytes 6291464 | tf_op jit(solution)/shard_map/ppermute | solution.py:385
  144.4 74.9 %collective-permute-start.13 = (bf16[1024,1024]{1,0:T(8,128)(2,1)}, bf16[1024,1024]{1,0:T(8,128)(2,1)}, u32[]{:S(2)}, u32[]{:S(2)}) collective-permute-start(bf16[1024,1024]{1,0:T(8,128)(2,1)} %maximum_select_fusion.4), channel_id=1, source_target_pairs={{0,2},{2,0},{4,6},{6,4},{8,10},{10,8},{12,14},{14,12},{16,18},{18,... | collective-permute-start | bytes 6291464 | tf_op jit(solution)/shard_map/ppermute | solution.py:385
  152.5 24.9 %slice-start.2 = ((s8[4587520]{0:T(1024)(128)(4,1)}), s8[4194304]{0:T(1024)(128)(4,1)S(1)}, s32[]{:S(2)}) async-start(s8[4587520]{0:T(1024)(128)(4,1)} %bitcast.145), calls=%async_computation.2 | async-start | bytes 8388608
  154.9 22.5 %slice-start.3 = ((s8[4587520]{0:T(1024)(128)(4,1)}), s8[393216]{0:T(1024)(128)(4,1)S(1)}, s32[]{:S(2)}) async-start(s8[4587520]{0:T(1024)(128)(4,1)} %bitcast.145), calls=%async_computation.3 | async-start | bytes 786432
  188.4 18.8 %copy-start.23 = (bf16[1120,1024]{1,0:T(8,128)(2,1)}, bf16[1120,1024]{1,0:T(8,128)(2,1)S(1)}, u32[]{:S(2)}) copy-start(bf16[1120,1024]{1,0:T(8,128)(2,1)S(1)} %add_convert_fusion.1) | copy-start | bytes 6881284
  241.5 19.0 %copy-start.25 = (bf16[1120,1024]{1,0:T(8,128)(2,1)}, bf16[1120,1024]{1,0:T(8,128)(2,1)S(1)}, u32[]{:S(2)}) copy-start(bf16[1120,1024]{1,0:T(8,128)(2,1)S(1)} %get-tuple-element.54) | copy-start | bytes 6881284
  304.3 22.1 %slice-start = ((s8[4587520]{0:T(1024)(128)(4,1)}), s8[4194304]{0:T(1024)(128)(4,1)S(1)}, s32[]{:S(2)}) async-start(s8[4587520]{0:T(1024)(128)(4,1)} %bitcast.143), calls=%async_computation | async-start | bytes 8388608
  341.2 28.6 %copy-start.3 = (bf16[1120,1024]{1,0:T(8,128)(2,1)S(1)}, bf16[1120,1024]{1,0:T(8,128)(2,1)}, u32[]{:S(2)}) copy-start(bf16[1120,1024]{1,0:T(8,128)(2,1)} %copy-done.2) | copy-start | bytes 6881284
  434.2 205.7 %collective-permute-start.14 = (f32[13312]{0:T(1024)S(1)}, f32[13312]{0:T(1024)S(1)}, u32[]{:S(2)}, u32[]{:S(2)}) collective-permute-start(f32[13312]{0:T(1024)S(1)} %fusion.57), channel_id=1, source_target_pairs={{0,1},{1,0},{2,3},{3,2},{4,5},{5,4},{6,7},{7,6},{8,9},{9,8},{10,11... | collective-permute-start | bytes 159752 | tf_op jit(solution)/shard_map/ppermute | solution.py:389
  639.9 4.9 collective-permute-start.15
  644.8 5.3 collective-permute-start.16
  650.2 6.9 %collective-permute-start.17 = (f32[13312]{0:T(1024)S(1)}, f32[13312]{0:T(1024)S(1)}, u32[]{:S(2)}, u32[]{:S(2)}) collective-permute-start(f32[13312]{0:T(1024)S(1)} %add.318), channel_id=1, source_target_pairs={{0,8},{2,10},{4,12},{6,14},{8,0},{10,2},{12,4},{14,6},{16,24},{18,... | collective-permute-start | bytes 159752 | tf_op jit(solution)/shard_map/ppermute | solution.py:385
  657.1 14.9 %collective-permute-start.18 = (f32[13312]{0:T(1024)S(1)}, f32[13312]{0:T(1024)S(1)}, u32[]{:S(2)}, u32[]{:S(2)}) collective-permute-start(f32[13312]{0:T(1024)S(1)} %add.319), channel_id=1, source_target_pairs={{0,16},{2,18},{4,20},{6,22},{8,24},{10,26},{12,28},{14,30},{16,0},... | collective-permute-start | bytes 159752 | tf_op jit(solution)/shard_map/ppermute | solution.py:385
  (55 other events, 303.1 us)

commit v2 on v0

--- a/solution.py
+++ b/solution.py
@@ -4,6 +4,8 @@
 import jax
 import jax.numpy as jnp
 from jax import lax
+from jax.experimental import pallas as pl
+from jax.experimental.pallas import tpu as pltpu
 from jax.sharding import PartitionSpec as P
 
 HD = 64
@@ -258,6 +260,645 @@
     )
 
 
+LOG2E = 1.4426950408889634
+HIDDEN = -1e30
+
+
+def dot_nt(a, b):
+    return lax.dot_general(a, b, (((1,), (1,)), ((), ())), preferred_element_type=jnp.float32)
+
+
+def dot_nn(a, b):
+    return lax.dot_general(a, b, (((1,), (0,)), ((), ())), preferred_element_type=jnp.float32)
+
+
+def dot_tn(a, b):
+    return lax.dot_general(a, b, (((0,), (0,)), ((), ())), preferred_element_type=jnp.float32)
+
+
+def attend_kernel(rows, bias_ref, q_ref, k_ref, v_ref, out_ref, weight_ref, inv_ref):
+    length = q_ref.shape[0]
+    bias = bias_ref[...]
+    lane = lax.broadcasted_iota(jnp.int32, (1, 2 * HD), 1)
+    keys = k_ref[...]
+    values = v_ref[...]
+    for first in range(0, length, rows):
+        part = pl.ds(first, rows)
+        queries = q_ref[part, :]
+        query_places = lax.broadcasted_iota(jnp.int32, (rows, length), 0) + first
+        key_places = lax.broadcasted_iota(jnp.int32, (rows, length), 1)
+        hide = jnp.where(key_places <= query_places, 0.0, bias)
+        outs, invs = [], []
+        for head in range(2):
+            mine = jnp.where((lane // HD) == head, queries, jnp.zeros_like(queries))
+            scores = dot_nt(mine, keys) + hide
+            top = jnp.max(scores, axis=1, keepdims=True)
+            weights = jnp.exp2((scores - top) * (relax_factor * LOG2E))
+            inv = 1.0 / jnp.sum(weights, axis=1, keepdims=True)
+            low = weights.astype(jnp.bfloat16)
+            weight_ref[head, part, :] = low
+            outs.append(dot_nn(low, values) * inv)
+            invs.append(inv)
+        out_ref[part, :] = jnp.where(lane < HD, outs[0], outs[1]).astype(jnp.bfloat16)
+        inv_ref[part, :] = jnp.where(lane < HD, invs[0], invs[1])
+
+
+def attend(queries, keys, values, bias):
+    length, width = queries.shape
+    pairs = width // (2 * HD)
+    column = pl.BlockSpec((length, 2 * HD), lambda i: (0, i))
+    return pl.pallas_call(
+        partial(attend_kernel, length // 2),
+        grid=(pairs,),
+        in_specs=[pl.BlockSpec((1, length), lambda i: (0, 0)), column, column, column],
+        out_specs=[column, pl.BlockSpec((2, length, length), lambda i: (i, 0, 0)), column],
+        out_shape=[
+            jax.ShapeDtypeStruct((length, width), jnp.bfloat16),
+            jax.ShapeDtypeStruct((2 * pairs, length, length), jnp.bfloat16),
+            jax.ShapeDtypeStruct((length, width), jnp.float32),
+        ],
+        compiler_params=pltpu.CompilerParams(vmem_limit_bytes=56 * 2**20),
+        cost_estimate=pl.CostEstimate(
+            flops=pairs * 6 * 10**9, bytes_accessed=pairs * 7 * 10**6, transcendentals=0
+        ),
+    )(bias, queries, keys, values)
+
+
+def flip(value, bit):
+    count = lax.axis_size("dp")
+    return lax.ppermute(value, "dp", [(i, i ^ bit) for i in range(count)])
+
+
+def cross(value):
+    return lax.ppermute(value, "mp", [(0, 1), (1, 0)])
+
+
+def block(value, index, count, axis):
+    size = value.shape[axis] // count
+    return lax.dynamic_slice_in_dim(value, index * size, size, axis)
+
+
+def low(value):
+    return value.astype(jnp.bfloat16)
+
+
+MESH = pl.DeviceIdType.MESH
+CHUNK = 128
+
+
+def remote(source, target, sems, index, device):
+    return pltpu.make_async_remote_copy(
+        src_ref=source,
+        dst_ref=target,
+        send_sem=sems.at[(0, *index)],
+        recv_sem=sems.at[(1, *index)],
+        device_id=device,
+        device_id_type=MESH,
+    )
+
+
+def aligned(start, size, unit=16):
+    return pl.ds(pl.multiple_of(start, unit), size)
+
+
+def wide(value):
+    return value.astype(jnp.float32)
+
+
+def back_kernel(
+    query_scale,
+    q_ref,
+    k_ref,
+    v_ref,
+    mixed_ref,
+    grad_ref,
+    inv_ref,
+    weight_ref,
+    w_ref,
+    first_ref,
+    tokens_ref,
+    residual_ref,
+    gain_ref,
+    small_ref,
+    g_down,
+    g_up,
+    g_out,
+    input_ref,
+    sums_ref,
+    t_down,
+    t_up,
+    t_out,
+    t_qkv,
+    ds_ref,
+    dqkv_ref,
+    d_first,
+    g_qkv,
+    columns_of,
+    small_out,
+    small_in,
+    mine,
+    core_in,
+    held,
+    x_out,
+    x_in,
+    y_out,
+    y_in,
+    z_out,
+    z_in,
+    last,
+    load_sem,
+    core_sem,
+    x_sem,
+    y_sem,
+    z_sem,
+    zz_sem,
+    yy_sem,
+    cc_sem,
+    keep_sem,
+    small_sem,
+):
+    now = pl.program_id(0)
+    place = lax.axis_index("dp")
+    turn = lax.axis_index("mp")
+    core, side, level = place % 2, (place // 2) % 2, place // 4
+    levels = lax.axis_size("dp") // 4
+    sibling = {"dp": place + 1 - 2 * core}
+    across = {"mp": 1 - turn}
+    beside = {"dp": place + 2 - 4 * side}
+    floors = [{"dp": (level + step) % levels * 4 + place % 4} for step in range(1, levels)]
+    half, piece = CHUNK // 2, CHUNK // 2 // levels
+    width = d_first.shape[1]
+    pairs = width // (2 * HD)
+    q_down, q_up, q_out = t_down.shape[0] // 2, t_up.shape[0] // 2, t_out.shape[0] // 2
+    wides = t_up.shape[1] // width
+    n_down, n_up, n_out = q_down // CHUNK, q_up // CHUNK * wides, q_out // CHUNK
+    n_head = t_qkv.shape[1] // 2 // CHUNK
+    s_up = n_down
+    s_out = s_up + n_up
+    s_qkv = s_out + n_out
+    chunks = s_qkv + 3 * n_head
+
+    @pl.when(now == 0)
+    def _():
+        barrier = pltpu.get_barrier_semaphore()
+        partners = [sibling, across, beside, *floors]
+        for partner in partners:
+            pl.semaphore_signal(barrier, inc=1, device_id=partner, device_id_type=MESH)
+        pl.semaphore_wait(barrier, len(partners))
+
+
+    def pick(chunk, action):
+        @pl.when(chunk < s_up)
+        def _():
+            action(
+                lambda group, which: g_down.at[
+                    aligned((2 * group + which) * q_down + chunk * CHUNK, CHUNK), :
+                ],
+                lambda which, first, size: t_down.at[aligned(which * q_down + chunk * CHUNK + first, size), :],
+            )
+
+        @pl.when((chunk >= s_up) & (chunk < s_out))
+        def _():
+            row = (chunk - s_up) // wides * CHUNK
+            column = (chunk - s_up) % wides * width
+            action(
+                lambda group, which: g_up.at[
+                    aligned(which * q_up + row, CHUNK), aligned(group * wides * width + column, width, 128)
+                ],
+                lambda which, first, size: t_up.at[
+                    aligned(which * q_up + row + first, size), aligned(column, width, 128)
+                ],
+            )
+
+        @pl.when((chunk >= s_out) & (chunk < s_qkv))
+        def _():
+            action(
+                lambda group, which: g_out.at[
+                    aligned((2 * group + which) * q_out + (chunk - s_out) * CHUNK, CHUNK), :
+                ],
+                lambda which, first, size: t_out.at[
+                    aligned(which * q_out + (chunk - s_out) * CHUNK + first, size), :
+                ],
+            )
+
+        @pl.when(chunk >= s_qkv)
+        def _():
+            kind = (chunk - s_qkv) // n_head
+            row = (chunk - s_qkv) % n_head * CHUNK
+            action(
+                lambda group, which: g_qkv.at[group, kind, aligned(which * n_head * CHUNK + row, CHUNK), :],
+                lambda which, first, size: t_qkv.at[kind, aligned(which * n_head * CHUNK + row + first, size), :],
+            )
+
+    def any_source(group, which):
+        return g_down.at[pl.ds(0, CHUNK), :]
+
+    def any_target(which, first, size):
+        return t_down.at[pl.ds(0, size), :]
+
+    def loads(source, slot):
+        copies = []
+        for index, group in enumerate((1, 0)):
+            copies.append(pltpu.make_async_copy(source(group, core), mine.at[index], load_sem.at[index]))
+            copies.append(
+                remote(source(group, 1 - core), core_in.at[slot, index], core_sem, (slot, index), sibling)
+            )
+        return copies
+
+    def x_copy(slot):
+        return remote(x_out, x_in.at[slot], x_sem, (slot,), across)
+
+    def y_copy(slot):
+        return remote(y_out.at[aligned((1 - side) * half, half)], y_in.at[slot], y_sem, (slot,), beside)
+
+    def z_copies(slot):
+        return [
+            remote(
+                z_out.at[aligned((level + step) % levels * piece, piece)],
+                z_in.at[slot, step - 1],
+                z_sem,
+                (slot, step - 1),
+                floors[step - 1],
+            )
+            for step in range(1, levels)
+        ]
+
+    def keep_copies(target, slot):
+        part = target(core, side * half + level * piece, piece)
+        copies = [pltpu.make_async_copy(last, part, keep_sem)]
+        for step in range(1, levels):
+            copies.append(remote(last, part, zz_sem, (slot, step - 1), floors[step - 1]))
+        return copies
+
+    def yy_copy(target, slot):
+        part = target(core, side * half, half)
+        return remote(part, part, yy_sem, (slot,), beside)
+
+    def cc_copy(target, slot):
+        part = target(core, 0, CHUNK)
+        return remote(part, part, cc_sem, (slot,), sibling)
+
+    def stage_7(chunk, slot):
+        cc_copy(any_target, slot).wait()
+
+    def stage_6(chunk, slot):
+        yy_copy(any_target, slot).wait()
+        pick(chunk, lambda source, target: cc_copy(target, slot).start())
+
+    def stage_5(chunk, slot):
+        for copy in keep_copies(any_target, slot):
+            copy.wait()
+        pick(chunk, lambda source, target: yy_copy(target, slot).start())
+
+    def stage_4(chunk, slot):
+        for copy in z_copies(slot):
+            copy.wait()
+        total = wide(z_out[aligned(level * piece, piece), :])
+        for step in range(1, levels):
+            total = total + wide(z_in[slot, step - 1])
+        last[...] = low(total)
+
+        def send(source, target):
+            for copy in keep_copies(target, slot):
+                copy.start()
+
+        pick(chunk, send)
+
+    def stage_3(chunk, slot):
+        y_copy(slot).wait()
+        z_out[...] = low(wide(y_out[aligned(side * half, half), :]) + wide(y_in[slot]))
+        for copy in z_copies(slot):
+            copy.start()
+
+    def stage_2(chunk, slot):
+        x_copy(slot).wait()
+        y_out[...] = low(held[...] + wide(x_in[slot]))
+        y_copy(slot).start()
+
+    def stage_1(chunk, slot):
+        for copy in loads(any_source, slot):
+            copy.wait()
+        x_out[...] = low(wide(mine[0]) + wide(core_in[slot, 0]))
+        x_copy(slot).start()
+        held[...] = wide(mine[1]) + wide(core_in[slot, 1])
+
+    def stage_0(chunk, slot):
+        def send(source, target):
+            for copy in loads(source, slot):
+                copy.start()
+
+        pick(chunk, send)
+
+    stages = [stage_0, stage_1, stage_2, stage_3, stage_4, stage_5, stage_6, stage_7]
+    for stage in reversed(range(len(stages))):
+        chunk = now - stage
+
+        @pl.when((chunk >= 0) & (chunk < chunks))
+        def _(stage=stage, chunk=chunk):
+            stages[stage](chunk, chunk % 2)
+
+
+    @pl.when(now < 2 * pairs)
+    def _():
+        head = now % 2
+        pair = now // 2
+        lane = lax.broadcasted_iota(jnp.int32, (1, 2 * HD), 1)
+        own = (lane // HD) == head
+        scaled = wide(grad_ref[...]) * inv_ref[...]
+        grad = jnp.where(own, scaled * relax_factor, 0.0).astype(jnp.bfloat16)
+        inner = jnp.sum(wide(grad) * wide(mixed_ref[...]), axis=1, keepdims=True)
+        d_probs = dot_nt(grad, v_ref[...])
+        ds_ref[...] = low(wide(weight_ref[0]) * (d_probs - inner))
+        dq = low(dot_nn(ds_ref[...], k_ref[...]) * query_scale)
+        dk = low(dot_tn(ds_ref[...], q_ref[...]))
+        dv = low(dot_tn(weight_ref[0], low(scaled)))
+        for index, value in enumerate((dq, dk, dv)):
+            part = pl.ds(index * 2 * HD, 2 * HD)
+            dqkv_ref[:, part] = jnp.where(own | (head == 0), value, dqkv_ref[:, part])
+
+        @pl.when(head == 1)
+        def _():
+            d_qkv = dqkv_ref[...]
+            grads = low(dot_tn(d_qkv, first_ref[...]))
+            group, start = pair // (pairs // 2), pair % (pairs // 2) * 2 * HD
+            for index in range(3):
+                g_qkv[group, index, aligned(start, 2 * HD), :] = grads[index * 2 * HD : (index + 1) * 2 * HD]
+            columns = jnp.sum(wide(d_qkv), axis=0, keepdims=True)
+            columns_of[group, 0:1, aligned(start, 2 * HD, 128)] = columns[:, : 2 * HD]
+            columns_of[group, 0:1, aligned(width // 2 + start, 2 * HD, 128)] = columns[:, 4 * HD :]
+            weights = jnp.concatenate([w_ref[0], w_ref[1], w_ref[2]], axis=1)
+            update = dot_nt(d_qkv, weights)
+
+            @pl.when(pair == 0)
+            def _():
+                d_first[...] = update
+
+            @pl.when(pair > 0)
+            def _():
+                d_first[...] += update
+
+    small_at = 2 * pairs
+
+    @pl.when(now == small_at)
+    def _():
+        normed, scale = standardize(wide(tokens_ref[...]))
+        errors = d_first[...]
+        input_ref[...] = residual_ref[...] + norm_back(errors, normed, scale, gain_ref[...])
+        small_out[0:1, :] = jnp.sum(errors * normed, axis=0, keepdims=True)
+        small_out[1:4, :] = small_ref[1:4, :]
+        small_out[4:5, :] = jnp.sum(errors, axis=0, keepdims=True)
+        small_out[5:10, :] = small_ref[5:10, :]
+        small_out[10:11, :] = columns_of[0, 0:1, :]
+        small_out[11:13, :] = small_ref[11:13, :]
+        small_out[13:14, :] = columns_of[1, 0:1, :]
+        small_out[14:16, :] = small_ref[14:16, :]
+
+
+    def small_copies(stage):
+        if stage < 3:
+            return [remote(small_out, small_in.at[stage], small_sem, (stage,), (sibling, across, beside)[stage])]
+        return [
+            remote(small_out, small_in.at[3 + level], small_sem, (2 + step,), floors[step - 1])
+            for step in range(1, levels)
+        ]
+
+    @pl.when(now == small_at)
+    def _():
+        small_copies(0)[0].start()
+
+    @pl.when(now == small_at + 1)
+    def _():
+        small_copies(0)[0].wait()
+        small_out[...] += small_in[0]
+        small_copies(1)[0].start()
+
+    @pl.when(now == small_at + 2)
+    def _():
+        small_copies(1)[0].wait()
+        small_out[0:10, :] += small_in[1, 0:10, :]
+        small_out[10:13, :] += small_in[1, 13:16, :]
+        small_copies(2)[0].start()
+
+    @pl.when(now == small_at + 3)
+    def _():
+        small_copies(2)[0].wait()
+        small_out[...] += small_in[2]
+        small_in[3 + level] = small_out[...]
+        for copy in small_copies(3):
+            copy.start()
+
+    @pl.when(now == small_at + 4)
+    def _():
+        for copy in small_copies(3):
+            copy.wait()
+        total = small_in[3]
+        for index in range(1, levels):
+            total = total + small_in[3 + index]
+        sums_ref[...] = total
+
+
+def back_all(queries, keys, values, mixed, grad, inv, weights, w_qkv, first, tokens, residual, gain, small, g_down, g_up, g_out, query_scale):
+    length, width = queries.shape
+    pairs = width // (2 * HD)
+    ff = g_down.shape[0]
+    levels = lax.axis_size("dp") // 4
+    half, piece = CHUNK // 2, CHUNK // 2 // levels
+    chunks = (ff // 4 + width // 2 * ff // 2 // width + width // 4 + 3 * width // 4) // CHUNK
+    kind, sem = jnp.bfloat16, pltpu.SemaphoreType.DMA
+    column = pl.BlockSpec((length, 2 * HD), lambda i: (0, jnp.minimum(i // 2, pairs - 1)))
+
+    def whole(shape):
+        return pl.BlockSpec(shape, lambda i: (0,) * len(shape), pipeline_mode=pl.Buffered(1))
+
+    hbm = pl.BlockSpec(memory_space=pl.ANY)
+    return pl.pallas_call(
+        partial(back_kernel, query_scale),
+        grid=(chunks + 7,),
+        in_specs=[
+            *[column] * 6,
+            pl.BlockSpec((1, length, length), lambda i: (jnp.minimum(i, 2 * pairs - 1), 0, 0)),
+            pl.BlockSpec((3, width, 2 * HD), lambda i: (0, 0, jnp.minimum(i // 2, pairs - 1))),
+            whole((length, width)),
+            whole((length, width)),
+            whole((length, width)),
+            whole((1, width)),
+            whole((16, width)),
+            hbm,
+            hbm,
+            hbm,
+        ],
+        out_specs=[
+            whole((length, width)),
+            whole((16, width)),
+            hbm,
+            hbm,
+            hbm,
+            hbm,
+        ],
+        out_shape=[
+            jax.ShapeDtypeStruct((length, width), jnp.float32),
+            jax.ShapeDtypeStruct((16, width), jnp.float32),
+            jax.ShapeDtypeStruct((ff // 2, width), kind),
+            jax.ShapeDtypeStruct((width, ff // 2), kind),
+            jax.ShapeDtypeStruct((width // 2, width), kind),
+            jax.ShapeDtypeStruct((3, width // 2, width), kind),
+        ],
+        scratch_shapes=[
+            pltpu.VMEM((length, length), kind),
+            pltpu.VMEM((length, 6 * HD), kind),
+            pltpu.VMEM((length, width), jnp.float32),
+            pltpu.VMEM((2, 3, width // 2, width), kind),
+            pltpu.VMEM((2, 8, width), jnp.float32),
+            pltpu.VMEM((16, width), jnp.float32),
+            pltpu.VMEM((3 + levels, 16, width), jnp.float32),
+            pltpu.VMEM((2, CHUNK, width), kind),
+            pltpu.VMEM((2, 2, CHUNK, width), kind),
+            pltpu.VMEM((CHUNK, width), jnp.float32),
+            pltpu.VMEM((CHUNK, width), kind),
+            pltpu.VMEM((2, CHUNK, width), kind),
+            pltpu.VMEM((CHUNK, width), kind),
+            pltpu.VMEM((2, half, width), kind),
+            pltpu.VMEM((half, width), kind),
+            pltpu.VMEM((2, levels - 1, piece, width), kind),
+            pltpu.VMEM((piece, width), kind),
+            sem((2,)),
+            sem((2, 2, 2)),
+            sem((2, 2)),
+            sem((2, 2)),
+            sem((2, 2, levels - 1)),
+            sem((2, 2, levels - 1)),
+            sem((2, 2)),
+            sem((2, 2)),
+            sem,
+            sem((2, 2 + levels)),
+        ],
+        compiler_params=pltpu.CompilerParams(
+            collective_id=0, has_side_effects=True, vmem_limit_bytes=60 * 2**20
+        ),
+    )(queries, keys, values, mixed, grad, inv, weights, w_qkv, first, tokens, residual, gain, small, g_down, g_up, g_out)
+
+
+def sequence_shards(
+    tokens,
+    cond_flags,
+    seg_lengths,
+    norm_gains,
+    norm_biases,
+    w_qkv,
+    qv_bias,
+    w_out,
+    out_biases,
+    w_up,
+    up_bias,
+    w_down,
+    cotangent,
+):
+    length, width = tokens.shape
+    place = lax.axis_index("dp")
+    turn = lax.axis_index("mp")
+    core = place % 2
+    side = (place // 2) % 2
+    query_scale = 1.0 / (relax_factor * math.sqrt(HD))
+
+    def in_order(which, mine, other, axis):
+        return jnp.where(
+            which == 0,
+            jnp.concatenate([mine, other], axis=axis),
+            jnp.concatenate([other, mine], axis=axis),
+        )
+
+    def fetch(weight, axis):
+        first = cross(block(weight, 2 * core + side, 4, axis))
+        near = in_order(side, first, flip(first, 2), axis)
+        return jnp.concatenate([weight, in_order(core, near, flip(near, 1), axis)], axis=axis)
+
+    w_qkv = fetch(w_qkv, 2)
+    w_out = fetch(w_out, 0)
+    w_up = fetch(w_up, 1)
+    w_down = fetch(w_down, 0)
+    qv_bias = jnp.concatenate([qv_bias, cross(qv_bias)], axis=1)
+    up_bias = jnp.concatenate([up_bias, cross(up_bias)])
+
+    marks = token_marks(
+        lax.dynamic_index_in_dim(cond_flags, turn, 0, keepdims=False),
+        lax.dynamic_index_in_dim(seg_lengths, turn, 0, keepdims=False),
+        length,
+    )
+    hide = jnp.where(marks[None, :] == 1, 0.0, HIDDEN).astype(jnp.float32)
+
+    source = tokens.astype(jnp.float32)
+    normed_one, scale_one = standardize(source)
+    first_in = low(normed_one * norm_gains[0] + norm_biases[0])
+    queries = low((dot_nn(first_in, w_qkv[0]) + qv_bias[0]) * query_scale)
+    keys = low(dot_nn(first_in, w_qkv[1]))
+    values = low(dot_nn(first_in, w_qkv[2]) + qv_bias[1])
+    mixed, kept, inv = attend(queries, keys, values, hide)
+    attended = out_biases[0] + dot_nn(mixed, w_out)
+    normed_two, scale_two = standardize(attended)
+    residual = source + normed_two * norm_gains[1] + norm_biases[1]
+    normed_three, scale_three = standardize(residual)
+    third_in = low(normed_three * norm_gains[2] + norm_biases[2])
+    up = dot_nn(third_in, w_up) + up_bias
+    act = low(jax.nn.gelu(up, approximate=True))
+    down = out_biases[1] + dot_nn(act, w_down)
+    normed_four, scale_four = standardize(down)
+    result = low(residual + normed_four * norm_gains[3] + norm_biases[3])
+    grad_out = cotangent.astype(jnp.float32)
+    d_down = norm_back(grad_out, normed_four, scale_four, norm_gains[3])
+    d_down_low = low(d_down)
+    pull = jax.vjp(partial(jax.nn.gelu, approximate=True), up)[1]
+    d_up = low(pull(dot_nt(d_down_low, w_down))[0])
+    g_down = low(dot_tn(act, d_down_low))
+    g_up = low(dot_tn(third_in, d_up))
+    d_third = dot_nt(d_up, w_up)
+    d_residual = grad_out + norm_back(d_third, normed_three, scale_three, norm_gains[2])
+    d_attended = norm_back(d_residual, normed_two, scale_two, norm_gains[1])
+    d_att_low = low(d_attended)
+    g_out = low(dot_tn(mixed, d_att_low))
+    d_mixed = low(dot_nt(d_att_low, w_out))
+
+    def rows(value):
+        return jnp.sum(value, axis=0, dtype=jnp.float32).reshape(-1, width)
+
+    blank = jnp.zeros((1, width), jnp.float32)
+    up_rows = rows(d_up)
+    small = jnp.concatenate(
+        [
+            blank,
+            rows(d_residual * normed_two),
+            rows(d_third * normed_three),
+            rows(grad_out * normed_four),
+            blank,
+            rows(d_residual),
+            rows(d_third),
+            rows(grad_out),
+            rows(d_attended),
+            rows(d_down),
+            blank,
+            up_rows[:2],
+            blank,
+            up_rows[2:],
+        ]
+    )
+    grad_input, sums, t_down, t_up, t_out, t_qkv = back_all(
+        queries, keys, values, mixed, d_mixed, inv, kept, w_qkv, first_in, tokens, d_residual,
+        norm_gains[:1], small, g_down, g_up, g_out, query_scale,
+    )
+    return (
+        result,
+        grad_input,
+        sums[:4],
+        sums[4:8],
+        t_qkv.astype(jnp.float32).transpose(0, 2, 1),
+        sums[10].reshape(2, -1),
+        t_out.astype(jnp.float32),
+        sums[8:10],
+        t_up.astype(jnp.float32),
+        sums[11:13].reshape(-1),
+        t_down.astype(jnp.float32),
+    )
+
+
 def solution(mesh):
     in_specs = (
         P(("dp", "mp"), None),
@@ -287,4 +928,13 @@
         P("mp"),
         P("mp", None),
     )
-    return jax.shard_map(shards, mesh=mesh, in_specs=in_specs, out_specs=out_specs, check_vma=False)
+    per_device = mesh.shape["dp"] * mesh.shape["mp"]
+
+    def step(*args):
+        whole_sequences = args[1].shape[0] == per_device
+        local = sequence_shards if whole_sequences and mesh.shape["mp"] == 2 and mesh.shape["dp"] == 16 else shards
+        return jax.shard_map(
+            local, mesh=mesh, in_specs=in_specs, out_specs=out_specs, check_vma=False
+        )(*args)
+
+    return step

time: 1610 us -> 595 us (0.37)
  waiting for transfers between devices: 762 us -> 58.7 us
  matrix products: 408 us -> 150 us
  Pallas kernels: 0 us -> 254 us
  local copies, waits for them, and re-layouts: 144 us -> 29.1 us
  other arithmetic: 174 us -> 78 us
  blocking collectives: 76.4 us -> 0 us
  loops' own time: 21.9 us -> 0 us
    reduce_scatter x4 -> x0, waiting for transfers between devices: 364 us -> none  [the longest x1 108 us: shards(): lax.psum_scatter(jnp.einsum('tf,df->td', d_up, w_up, preferred_element_ty...]
    dot_general x40 -> x12, matrix products: 408 us -> 150 us  [the longest x6 56.2 us: dot_nn(): lax.dot_general(a, b, (((1,), (0,)), ((), ())), preferred_element_type=jn...]
    pallas_call x0 -> x2, Pallas kernels: none -> 254 us  [the longest x1 213 us: back_all(): pl.pallas_call(partial(back_kernel, query_scale), grid=(chunks + 7,), in_...]
    all_gather x4 -> x0, waiting for transfers between devices: 217 us -> none  [the longest x1 63.3 us: shards(): first_all = lax.all_gather(first_in, 'mp', axis=0, tiled=True)]
    psum x1 -> x0, waiting for transfers between devices: 182 us -> none  [shards(): lax.psum(grad_w_qkv.astype(jnp.bfloat16), 'dp').astype(jnp.float32)]
    psum x2 -> x0, blocking collectives: 76.4 us -> none  [the longest x1 40.3 us: shards(): lax.psum((gain_sums, bias_sums, outer_sums), ('dp', 'mp'))]
    convert_element_type x12 -> x4, other arithmetic: 78.8 us -> 15.1 us  [the longest x1 6.8 us: sequence_shards(): t_up.astype(jnp.float32)]
    ppermute x0 -> x14, waiting for transfers between devices: none -> 58.7 us  [the longest x6 33.6 us: cross(): return lax.ppermute(value, 'mp', [(0, 1), (1, 0)])]
  transfers between devices with their start and end apart: 9 -> 14, of which waited for: 9 -> 6; matrix products, arithmetic and copies ran while one was open for 4% -> 13% of each run, Pallas kernels for 0% -> 7%
where the time goes in v2:
time: 595 us; the launch traced here: 588 us
  Pallas kernels  254 us (43%)
  matrix products  150 us (25%)
  other arithmetic  78 us (13%)
  waiting for transfers between devices  58.7 us (10%)
  local copies, waits for them, and re-layouts  29.1 us (5%)
  starting transfers between devices  15.3 us (3%)
    pallas_call x1, Pallas kernels, back_all(): pl.pallas_call(partial(back_kernel, query_scale), grid=(chunks + 7,), in_...  213 us
    dot_general x6, matrix products, dot_nn(): lax.dot_general(a, b, (((1,), (0,)), ((), ())), preferred_element_type=jn...  56.2 us
    dot_general x3, matrix products, dot_nt(): lax.dot_general(a, b, (((1,), (1,)), ((), ())), preferred_element_type=jn...  49.6 us
    dot_general x3, matrix products, dot_tn(): lax.dot_general(a, b, (((0,), (0,)), ((), ())), preferred_element_type=jn...  43.8 us
    pallas_call x1, Pallas kernels, attend(): pl.pallas_call(partial(attend_kernel, length // 2), grid=(pairs,), in_spe...  41.1 us
    ppermute x6, waiting for transfers between devices, cross(): return lax.ppermute(value, 'mp', [(0, 1), (1, 0)])  33.6 us
    select_n x8, other arithmetic, in_order(): jnp.where(which == 0, jnp.concatenate([mine, other], axis=axis), jnp.conc...  29.3 us
    ppermute x8, waiting for transfers between devices, flip(): return lax.ppermute(value, 'dp', [(i, i ^ bit) for i in range(count)])  25.1 us
  transfers between devices with their start and end apart: 14, of which 6 were waited for; matrix products, arithmetic and copies ran while one was open for 13% of the time, Pallas kernels for 7%

profile of v2, /device:TPU:0, one launch (start us, length us, event | category | flops | bytes accessed | tf_op | source)
XLA Modules:
  0.0 588.1 jit_solution(15112834280118918562)
XLA Ops:
  16.5 8.0 %collective-permute-done = bf16[3,1024,128]{2,1,0:T(8,128)(2,1)} collective-permute-done((bf16[3,1024,128]{2,1,0:T(8,128)(2,1)}, bf16[3,1024,128]{2,1,0:T(8,128)(2,1)}, u32[]{:S(2)}, u32[]{:S(2)}) %collective-permute-start) | collective-permute-done | bytes 786464 | tf_op jit(solution)/shard_map/ppermute | solution.py:333
  32.4 13.1 %collective-permute-done.1 = bf16[3,1024,128]{2,1,0:T(8,128)(2,1)} collective-permute-done((bf16[3,1024,128]{2,1,0:T(8,128)(2,1)}, bf16[3,1024,128]{2,1,0:T(8,128)(2,1)}, u32[]{:S(2)}, u32[]{:S(2)}) %collective-permute-start.1) | collective-permute-done | bytes 786464 | tf_op jit(solution)/shard_map/ppermute | solution.py:329
  45.4 3.5 maximum_select_fusion.5
  48.9 3.8 collective-permute-done.7
  54.8 19.6 %collective-permute-done.11 = bf16[512,1024]{1,0:T(8,128)(2,1)} collective-permute-done((bf16[512,1024]{1,0:T(8,128)(2,1)S(1)}, bf16[512,1024]{1,0:T(8,128)(2,1)}, u32[]{:S(2)}, u32[]{:S(2)}) %collective-permute-start.11) | collective-permute-done | bytes 1048608 | tf_op jit(solution)/shard_map/ppermute | solution.py:333
  82.3 4.7 maximum_select_fusion.3
  87.0 12.1 %collective-permute-done.12 = bf16[512,1024]{1,0:T(8,128)(2,1)} collective-permute-done((bf16[512,1024]{1,0:T(8,128)(2,1)}, bf16[512,1024]{1,0:T(8,128)(2,1)}, u32[]{:S(2)}, u32[]{:S(2)}) %collective-permute-start.12) | collective-permute-done | bytes 1048608 | tf_op jit(solution)/shard_map/ppermute | solution.py:329
  99.0 4.7 maximum_select_fusion.4
  103.8 3.9 maximum_select_fusion.2
  107.7 3.9 convolution_convert_fusion.3.k_ref
  111.6 4.0 add_convert_fusion.2.v_ref
  115.5 4.0 multiply_convert_fusion.1.q_ref
  119.5 41.1 %shard_map.212 = (bf16[1120,1024]{1,0:T(8,128)(2,1)}, bf16[16,1120,1120]{2,1,0:T(8,128)(2,1)}, f32[1120,1024]{1,0:T(8,128)}) custom-call(f32[1,1120]{1,0:T(1,128)} %select_n.96.bias_ref, bf16[1120,1024]{1,0:T(8,128)(2,1)} %multiply_convert_fusion.1.q_ref, bf16[1120,1024]{1,0:T(8,128)(2,1)} %convolution_convert_fusion.3.k_ref, ...), custom_call_target="tpu_custom_call" | custom-call | flops 48000000000 | bytes 56000000 | tf_op jit(solution)/shard_map/pallas_call | solution.py:310
  160.6 4.3 fusion.67
  167.1 7.2 %pad_maximum_fusion.w_ref = bf16[3,1024,1024]{2,1,0:T(8,128)(2,1)} fusion(bf16[3,1024,512]{2,1,0:T(8,128)(2,1)S(1)} %maximum_select_fusion.2, bf16[3,1024,512]{2,1,0:T(8,128)(2,1)} %param.18), kind=kLoop, calls=%fused_computation.14 | loop fusion | flops 12582912 | bytes 12582912 | tf_op jit(solution)/shard_map/concatenate | solution.py:813
  174.9 5.0 maximum_select_fusion
  179.9 17.4 %fusion.15 = f32[1120,4096]{1,0:T(8,128)} fusion(bf16[1024,2048]{1,0:T(8,128)(2,1)S(1)} %maximum_select_fusion, bf16[1024,2048]{1,0:T(8,128)(2,1)} %param.22, f32[1120,1024]{1,0:T(8,128)S(1)} %get-tuple-element.69, f32[1024]{0:T(1024)S(1)} %bitcast.83, f32[1024]{0:T(1024)S(1)} %bitcast.68, f32[1120]{0:T(1024)S(1)} %add_rsqrt_fusion.1, ...), kind=kOutput, calls=%fused_computation.38 | convolution fusion | flops 9417752576 | bytes 31343360 | tf_op jit(solution)/shard_map/dot_general | solution.py:272
  197.3 5.8 maximum_select_fusion.1
  203.2 22.6 %fusion.68 = (f32[1120]{0:T(1024)S(1)}, f32[1120,1024]{1,0:T(8,128)}) fusion(bf16[2048,1024]{1,0:T(8,128)(2,1)} %maximum_select_fusion.1, bf16[2048,1024]{1,0:T(8,128)(2,1)} %param.24, f32[1120,4096]{1,0:T(8,128)} %fusion.15, f32[4096]{0:T(1024)S(1)} %pad_maximum_fusion.14, f32[1024]{0:T(1024)S(1)} %bitcast.79), kind=kOutput, calls=%fused_computation.144 | convolution fusion | flops 9460186112 | bytes 31351168 | tf_op jit(solution)/shard_map/dot_general | solution.py:272
  235.2 28.3 %convert_reduce_fusion = (f32[4096]{0:T(1024)S(1)}, bf16[1120,4096]{1,0:T(8,128)(2,1)}) fusion(f32[1120,4096]{1,0:T(8,128)} %fusion.15, f32[4096]{0:T(1024)S(1)} %pad_maximum_fusion.14, bf16[2048,1024]{1,0:T(8,128)(2,1)S(1)} %copy-done.14, bf16[2048,1024]{1,0:T(8,128)(2,1)} %param.24, bf16[1120,1024]{1,0:T(8,128)(2,1)S(1)} %get-tuple-element.64), kind=kOutput, calls=%fused_computation.9 | convolution fusion | flops 9517527040 | bytes 38240256 | tf_op jit(solution)/shard_map/dot_general | solution.py:268
  263.6 17.2 %multiply_reduce_fusion = (f32[1024]{0:T(1024)S(1)}, f32[1120]{0:T(1024)S(1)}, f32[1120]{0:T(1024)S(1)}, f32[1024]{0:T(1024)S(1)}, f32[1120,1024]{1,0:T(8,128)}) fusion(f32[1120,1024]{1,0:T(8,128)S(1)} %copy-done.4, f32[1120]{0:T(1024)S(1)} %add_rsqrt_fusion.1, f32[1120]{0:T(1024)S(1)} %broadcast_multiply_fusion.7, f32[1024]{0:T(1024)S(1)} %bitcast.69, ...), kind=kOutput, calls=%fused_computation.48 | convolution fusion | flops 9422336000 | bytes 26768896 | tf_op jit(solution)/shard_map/dot_general | solution.py:268
  280.8 17.7 %convolution_convert_fusion.g_up = bf16[1024,4096]{1,0:T(8,128)(2,1)} fusion(bf16[1120,4096]{1,0:T(8,128)(2,1)} %get-tuple-element.97, f32[1120,1024]{1,0:T(8,128)S(1)} %copy-done.4, f32[1024]{0:T(1024)S(1)} %bitcast.84, f32[1024]{0:T(1024)S(1)} %bitcast.70, f32[1120]{0:T(1024)S(1)} %add_rsqrt_fusion.1, f32[1120]{0:T(1024)S(1)} %broadcast_multiply_fusion.7), kind=kOutput, calls=%fused_computation.24 | convolution fusion | flops 9405169664 | bytes 22168320 | tf_op jit(solution)/shard_map/dot_general | solution.py:276
  298.5 22.0 %convolution_convert_fusion.1.g_down = bf16[4096,1024]{1,0:T(8,128)(2,1)} fusion(bf16[1120,1024]{1,0:T(8,128)(2,1)} %copy-done.15, f32[1120,4096]{1,0:T(8,128)} %fusion.15, f32[4096]{0:T(1024)S(1)} %pad_maximum_fusion.14), kind=kOutput, calls=%fused_computation.25 | convolution fusion | flops 9445310464 | bytes 29048832 | tf_op jit(solution)/shard_map/dot_general | solution.py:276
  320.5 6.2 %multiply_reduce_fusion.1 = (f32[1024]{0:T(1024)S(1)}, f32[1120]{0:T(1024)S(1)}, f32[1120]{0:T(1024)S(1)}, f32[1024]{0:T(1024)S(1)}, f32[1120,1024]{1,0:T(8,128)S(1)}) fusion(f32[1120,1024]{1,0:T(8,128)S(1)} %bitcast.56, f32[1120]{0:T(1024)S(1)} %copy-done.23, f32[1120]{0:T(1024)S(1)} %copy-done.21, f32[1024]{0:T(1024)S(1)} %bitcast.58, ...), kind=kLoop, calls=%fused_computation.49 | loop fusion | flops 20639552 | bytes 20696064 | tf_op jit(solution)/shard_map/reduce_sum | solution.py:861
  330.0 4.1 convolution_convert_fusion.4.g_out
  334.2 4.0 convolution_convert_fusion.2.grad_ref
  339.6 213.4 %shard_map.213 = (f32[1120,1024]{1,0:T(8,128)}, f32[16,1024]{1,0:T(8,128)}, bf16[2048,1024]{1,0:T(8,128)(2,1)}, bf16[1024,2048]{1,0:T(8,128)(2,1)}, bf16[512,102...) custom-call(bf16[1120,1024]{1,0:T(8,128)(2,1)} %multiply_convert_fusion.1.q_ref, ...), custom_call_target="tpu_custom_call" | custom-call | tf_op jit(solution)/shard_map/pallas_call | solution.py:714
  556.6 5.3 convert_bitcast_fusion
  562.0 6.6 %copy.25 = f32[3,1024,512]{2,1,0:T(8,128)} copy(f32[3,1024,512]{1,2,0:T(8,128)} %convert_bitcast_fusion) | data formatting | bytes 12582912
  568.5 6.8 %convert_element_type.96 = f32[1024,2048]{1,0:T(8,128)} convert(bf16[1024,2048]{1,0:T(8,128)(2,1)} %get-tuple-element.27) | non-fusion elementwise | flops 2097152 | bytes 12582912 | tf_op jit(solution)/shard_map/convert_element_type | solution.py:896
  575.3 4.4 convert_element_type.97
  582.5 5.1 copy.31
  (152 shorter events, 55.4 us)
Async XLA Ops:
  0.6 28.4 %copy-start = (s32[2,3]{1,0:T(2,128)S(1)}, s32[2,3]{1,0:T(2,128)}, u32[]{:S(2)}) copy-start(s32[2,3]{1,0:T(2,128)} %param.15) | copy-start | bytes 76
  2.9 21.6 %collective-permute-start = (bf16[3,1024,128]{2,1,0:T(8,128)(2,1)}, bf16[3,1024,128]{2,1,0:T(8,128)(2,1)}, u32[]{:S(2)}, u32[]{:S(2)}) collective-permute-start(bf16[3,1024,128]{2,1,0:T(8,128)(2,1)} %constant_dynamic-slice_fusion.2), channel_id=1, source_target_pairs={{0,1},{1,0},{2,3},{3,2},{4,5},{5,4},{6,7},{7,6},{8,9},{9,8},{10,11... | collective-permute-start | bytes 2359304 | tf_op jit(solution)/shard_map/ppermute | solution.py:333
  5.9 72.2 %collective-permute-start.3 = (f32[2,512]{1,0:T(2,128)}, f32[2,512]{1,0:T(2,128)S(1)}, u32[]{:S(2)}, u32[]{:S(2)}) collective-permute-start(f32[2,512]{1,0:T(2,128)} %param.19), channel_id=1, source_target_pairs={{0,1},{1,0},{2,3},{3,2},{4,5},{5,4},{6,7},{7,6},{8,9},{9,8},{10,11... | collective-permute-start | bytes 12296 | tf_op jit(solution)/shard_map/ppermute | solution.py:333
  7.6 24.0 %collective-permute-start.4 = (bf16[128,1024]{1,0:T(8,128)(2,1)}, bf16[128,1024]{1,0:T(8,128)(2,1)}, u32[]{:S(2)}, u32[]{:S(2)}) collective-permute-start(bf16[128,1024]{1,0:T(8,128)(2,1)} %constant_dynamic-slice_fusion.1), channel_id=1, source_target_pairs={{0,1},{1,0},{2,3},{3,2},{4,5},{5,4},{6,7},{7,6},{8,9},{9,8},{10,11... | collective-permute-start | bytes 786440 | tf_op jit(solution)/shard_map/ppermute | solution.py:333
  11.8 40.9 %collective-permute-start.7 = (bf16[1024,512]{1,0:T(8,128)(2,1)}, bf16[1024,512]{1,0:T(8,128)(2,1)}, u32[]{:S(2)}, u32[]{:S(2)}) collective-permute-start(bf16[1024,512]{1,0:T(8,128)(2,1)} %constant_dynamic-slice_fusion), channel_id=1, source_target_pairs={{0,1},{1,0},{2,3},{3,2},{4,5},{5,4},{6,7},{7,6},{8,9},{9,8},{10,11... | collective-permute-start | bytes 3145736 | tf_op jit(solution)/shard_map/ppermute | solution.py:333
  13.2 61.2 %collective-permute-start.11 = (bf16[512,1024]{1,0:T(8,128)(2,1)S(1)}, bf16[512,1024]{1,0:T(8,128)(2,1)}, u32[]{:S(2)}, u32[]{:S(2)}) collective-permute-start(bf16[512,1024]{1,0:T(8,128)(2,1)S(1)} %constant_dynamic-slice_fusion.3), channel_id=1, source_target_pairs={{0,1},{1,0},{2,3},{3,2},{4,5},{5,4},{6,7},{7,6},{8,9},{9,8},{10,11... | collective-permute-start | bytes 3145736 | tf_op jit(solution)/shard_map/ppermute | solution.py:333
  15.6 60.5 %copy-start.31 = (f32[2,1024]{1,0:T(2,128)S(1)}, f32[2,1024]{1,0:T(2,128)}, u32[]{:S(2)}) copy-start(f32[2,1024]{1,0:T(2,128)} %param.21) | copy-start | bytes 24580
  16.4 61.1 %copy-start.33 = (f32[2,512]{1,0:T(2,128)S(1)}, f32[2,512]{1,0:T(2,128)}, u32[]{:S(2)}) copy-start(f32[2,512]{1,0:T(2,128)} %param.19) | copy-start | bytes 12292
  16.4 61.7 %copy-start.32 = (f32[2048]{0:T(1024)S(1)}, f32[2048]{0:T(1024)}, u32[]{:S(2)}) copy-start(f32[2048]{0:T(1024)} %param.23) | copy-start | bytes 24580
  16.5 149.1 %copy-start.24 = (f32[1,1024]{1,0:T(1,128)}, f32[1,1024]{1,0:T(1,128)S(1)}, u32[]{:S(2)}) copy-start(f32[1,1024]{1,0:T(1,128)S(1)} %get-tuple-element.78) | copy-start | bytes 12292
  24.6 20.9 %collective-permute-start.1 = (bf16[3,1024,128]{2,1,0:T(8,128)(2,1)}, bf16[3,1024,128]{2,1,0:T(8,128)(2,1)}, u32[]{:S(2)}, u32[]{:S(2)}) collective-permute-start(bf16[3,1024,128]{2,1,0:T(8,128)(2,1)} %collective-permute-done), channel_id=1, source_target_pairs={{0,4},{2,6},{4,0},{6,2},{8,12},{10,14},{12,8},{14,10},{16,20},{18,... | collective-permute-start | bytes 2359304 | tf_op jit(solution)/shard_map/ppermute | solution.py:329
  31.7 44.5 %collective-permute-start.5 = (bf16[128,1024]{1,0:T(8,128)(2,1)}, bf16[128,1024]{1,0:T(8,128)(2,1)S(1)}, u32[]{:S(2)}, u32[]{:S(2)}) collective-permute-start(bf16[128,1024]{1,0:T(8,128)(2,1)} %collective-permute-done.4), channel_id=1, source_target_pairs={{0,4},{2,6},{4,0},{6,2},{8,12},{10,14},{12,8},{14,10},{16,20},{18,... | collective-permute-start | bytes 786440 | tf_op jit(solution)/shard_map/ppermute | solution.py:329
  48.9 54.9 %collective-permute-start.2 = (bf16[3,1024,256]{2,1,0:T(8,128)(2,1)}, bf16[3,1024,256]{2,1,0:T(8,128)(2,1)}, u32[]{:S(2)}, u32[]{:S(2)}) collective-permute-start(bf16[3,1024,256]{2,1,0:T(8,128)(2,1)} %maximum_select_fusion.5), channel_id=1, source_target_pairs={{0,2},{2,0},{4,6},{6,4},{8,10},{10,8},{12,14},{14,12},{16,18},{18,... | collective-permute-start | bytes 4718600 | tf_op jit(solution)/shard_map/ppermute | solution.py:329
  52.7 29.5 %collective-permute-start.8 = (bf16[1024,512]{1,0:T(8,128)(2,1)}, bf16[1024,512]{1,0:T(8,128)(2,1)}, u32[]{:S(2)}, u32[]{:S(2)}) collective-permute-start(bf16[1024,512]{1,0:T(8,128)(2,1)} %collective-permute-done.7), channel_id=1, source_target_pairs={{0,4},{2,6},{4,0},{6,2},{8,12},{10,14},{12,8},{14,10},{16,20},{18,... | collective-permute-start | bytes 3145736 | tf_op jit(solution)/shard_map/ppermute | solution.py:329
  74.4 24.7 %collective-permute-start.12 = (bf16[512,1024]{1,0:T(8,128)(2,1)}, bf16[512,1024]{1,0:T(8,128)(2,1)}, u32[]{:S(2)}, u32[]{:S(2)}) collective-permute-start(bf16[512,1024]{1,0:T(8,128)(2,1)} %collective-permute-done.11), channel_id=1, source_target_pairs={{0,4},{2,6},{4,0},{6,2},{8,12},{10,14},{12,8},{14,10},{16,20},{18,... | collective-permute-start | bytes 3145736 | tf_op jit(solution)/shard_map/ppermute | solution.py:329
  77.4 4.4 collective-permute-start.6
  78.1 3.7 collective-permute-start.10
  82.3 78.3 %copy-start.18 = (bf16[512,1024]{1,0:T(8,128)(2,1)}, bf16[512,1024]{1,0:T(8,128)(2,1)S(1)}, u32[]{:S(2)}) copy-start(bf16[512,1024]{1,0:T(8,128)(2,1)S(1)} %maximum_select_fusion.6) | copy-start | bytes 3145732
  87.0 20.7 %copy-start.9 = (bf16[1120,1024]{1,0:T(8,128)(2,1)S(1)}, bf16[1120,1024]{1,0:T(8,128)(2,1)}, u32[]{:S(2)}) copy-start(bf16[1120,1024]{1,0:T(8,128)(2,1)} %fusion.19.first_ref) | copy-start | bytes 6881284
  87.0 20.7 %copy-start.10 = (bf16[3,1024,512]{2,1,0:T(8,128)(2,1)S(1)}, bf16[3,1024,512]{2,1,0:T(8,128)(2,1)}, u32[]{:S(2)}) copy-start(bf16[3,1024,512]{2,1,0:T(8,128)(2,1)} %param.18) | copy-start | bytes 9437188
  87.0 87.9 %collective-permute-start.9 = (bf16[1024,1024]{1,0:T(8,128)(2,1)}, bf16[1024,1024]{1,0:T(8,128)(2,1)}, u32[]{:S(2)}, u32[]{:S(2)}) collective-permute-start(bf16[1024,1024]{1,0:T(8,128)(2,1)} %maximum_select_fusion.3), channel_id=1, source_target_pairs={{0,2},{2,0},{4,6},{6,4},{8,10},{10,8},{12,14},{14,12},{16,18},{18,... | collective-permute-start | bytes 6291464 | tf_op jit(solution)/shard_map/ppermute | solution.py:329
  103.8 93.6 %collective-permute-start.13 = (bf16[1024,1024]{1,0:T(8,128)(2,1)}, bf16[1024,1024]{1,0:T(8,128)(2,1)}, u32[]{:S(2)}, u32[]{:S(2)}) collective-permute-start(bf16[1024,1024]{1,0:T(8,128)(2,1)} %maximum_select_fusion.4), channel_id=1, source_target_pairs={{0,2},{2,0},{4,6},{6,4},{8,10},{10,8},{12,14},{14,12},{16,18},{18,... | collective-permute-start | bytes 6291464 | tf_op jit(solution)/shard_map/ppermute | solution.py:329
  119.5 41.1 %copy-start.26 = (bf16[512,1024]{1,0:T(8,128)(2,1)S(1)}, bf16[512,1024]{1,0:T(8,128)(2,1)}, u32[]{:S(2)}) copy-start(bf16[512,1024]{1,0:T(8,128)(2,1)} %param.20) | copy-start | bytes 3145732
  179.9 17.4 %copy-start.12 = (bf16[1024,2048]{1,0:T(8,128)(2,1)}, bf16[1024,2048]{1,0:T(8,128)(2,1)S(1)}, u32[]{:S(2)}) copy-start(bf16[1024,2048]{1,0:T(8,128)(2,1)S(1)} %maximum_select_fusion) | copy-start | bytes 12582916
  203.2 25.7 %copy-start.8 = (bf16[1120,1024]{1,0:T(8,128)(2,1)S(1)}, bf16[1120,1024]{1,0:T(8,128)(2,1)}, u32[]{:S(2)}) copy-start(bf16[1120,1024]{1,0:T(8,128)(2,1)} %param.25) | copy-start | bytes 6881284
  235.2 28.3 %copy-start.15 = (bf16[1120,1024]{1,0:T(8,128)(2,1)}, bf16[1120,1024]{1,0:T(8,128)(2,1)S(1)}, u32[]{:S(2)}) copy-start(bf16[1120,1024]{1,0:T(8,128)(2,1)S(1)} %get-tuple-element.64) | copy-start | bytes 6881284
  235.2 28.3 %copy-start.13 = (bf16[1024,2048]{1,0:T(8,128)(2,1)S(1)}, bf16[1024,2048]{1,0:T(8,128)(2,1)}, u32[]{:S(2)}) copy-start(bf16[1024,2048]{1,0:T(8,128)(2,1)} %copy-done.12) | copy-start | bytes 12582916
  280.8 39.7 %slice-start = ((s8[4587520]{0:T(1024)(128)(4,1)}), s8[4194304]{0:T(1024)(128)(4,1)S(1)}, s32[]{:S(2)}) async-start(s8[4587520]{0:T(1024)(128)(4,1)} %bitcast.55), calls=%async_computation | async-start | bytes 8388608
  298.5 22.0 %slice-start.1 = ((s8[4587520]{0:T(1024)(128)(4,1)}), s8[393216]{0:T(1024)(128)(4,1)S(1)}, s32[]{:S(2)}) async-start(s8[4587520]{0:T(1024)(128)(4,1)} %bitcast.55), calls=%async_computation.1 | async-start | bytes 786432
  298.5 22.0 %copy-start.21 = (f32[1120]{0:T(1024)S(1)}, f32[1120]{0:T(1024)}, u32[]{:S(2)}) copy-start(f32[1120]{0:T(1024)} %copy-done.20) | copy-start | bytes 13444
  298.5 22.0 %copy-start.23 = (f32[1120]{0:T(1024)S(1)}, f32[1120]{0:T(1024)}, u32[]{:S(2)}) copy-start(f32[1120]{0:T(1024)} %copy-done.22) | copy-start | bytes 13444
  298.5 22.0 %copy-start.25 = (f32[1,1024]{1,0:T(1,128)S(1)}, f32[1,1024]{1,0:T(1,128)}, u32[]{:S(2)}) copy-start(f32[1,1024]{1,0:T(1,128)} %copy-done.24) | copy-start | bytes 12292
  (19 other events, 127.2 us)
